TPU v7x, 256 devices: a whole 4x4x8 slice. The times are simulated.
256 devices in a mesh: dp: 32 (over x, z), mp: 8 (over y, core).
Axes of the slice: x: 4, y: 4, z: 8, core: 2. Of those that a mesh axis runs over, the one named last changes fastest.
Arguments:
- train_inputs: bfloat16 [96, 320, 27648], P('dp', None, 'mp'), may hold values from -6 to 6
- train_grads_out: bfloat16 [96, 320, 5120], P('dp', None, 'mp'), may hold values from -6 to 6
- query_inputs: bfloat16 [32, 320, 27648], P('dp', None, 'mp'), may hold values from -6 to 6
- query_grads_out: bfloat16 [32, 320, 5120], P('dp', None, 'mp'), may hold values from -6 to 6
- proj_in: bfloat16 [27648, 256], P('mp'), may hold values from -0.0390625 to 0.0390625
- proj_out: bfloat16 [5120, 256], P('mp'), may hold values from -0.078125 to 0.078125
- out_inverse: float32 [256, 256], replicated, as said below
- in_inverse: float32 [256, 256], replicated, as said below
Outputs:
- scores: float32 [32, 96], P(None, 'dp')
Inputs may be any that keep to these rules, and one draw needn't show every extreme that they name: `out_inverse`: each row's diagonal entry lies between 0.5 and 4; the matrix is not symmetric. `in_inverse`: each row's diagonal entry lies between 0.5 and 4; the matrix is not symmetric.
All inputs are finite; a program needn't handle non-finite values.
Results may differ from a plain program's by a relative error of at most 0.0003.
Values sent between devices are 32-bit elements; how exact they have to be, the bound alone decides.
No kernel may reach another device: no remote copies, remote signals or barrier semaphores. Data moves between devices by JAX's collectives and lax.ppermute only.
A program may use at most 64 MiB of HBM per device.

v0:
```python
import jax
import jax.numpy as jnp
from jax import lax
from jax.sharding import PartitionSpec as P


def project(acts, weights):
    flat = acts.reshape(acts.shape[0] * acts.shape[1], acts.shape[2])
    result = jnp.dot(flat, weights, preferred_element_type=jnp.float32)
    return result.reshape(acts.shape[0], acts.shape[1], weights.shape[1])


def body(
    train_inputs,
    train_grads_out,
    query_inputs,
    query_grads_out,
    proj_in,
    proj_out,
    out_inverse,
    in_inverse,
):
    highest = lax.Precision.HIGHEST
    factor = train_inputs.shape[1] ** (-0.5)
    n_train = train_inputs.shape[0]
    width = proj_in.shape[1]
    train_x = project(train_inputs, proj_in)
    query_x = project(query_inputs, proj_in)
    train_y = project(train_grads_out, proj_out)
    query_y = project(query_grads_out, proj_out)
    in_side, out_side = lax.psum(
        (jnp.concatenate([train_x, query_x], 0), jnp.concatenate([train_y, query_y], 0)), "mp"
    )
    every_grad = jnp.einsum("sli,slj->sij", out_side, in_side, precision=highest) * factor
    train_grad = every_grad[:n_train]
    left = jnp.einsum("ik,qkj->qij", out_inverse, every_grad[n_train:], precision=highest)
    precond = jnp.einsum("qik,kj->qij", left, in_inverse, precision=highest)
    return (
        jnp.einsum(
            "qij,sij->qs",
            lax.all_gather(precond, "dp", axis=0, tiled=True),
            train_grad,
            precision=highest,
        )
        / width
    )


def solution(mesh):
    return jax.shard_map(
        body,
        mesh=mesh,
        in_specs=(
            P("dp", None, "mp"),
            P("dp", None, "mp"),
            P("dp", None, "mp"),
            P("dp", None, "mp"),
            P("mp", None),
            P("mp", None),
            P(),
            P(),
        ),
        out_specs=P(None, "dp"),
        check_vma=False,
    )
```

profile of v0, /device:TPU:1, one launch (start us, length us, event | category | flops | bytes accessed | tf_op | source)
XLA Modules:
  0.0 221.6 jit_solution(1139861986638212956)
XLA Ops:
  6.5 0.0 copy-start
  6.5 0.0 all-reduce.3.cloned.1.call-start
  6.5 1.6 copy-done
  8.2 0.0 copy-start.7
  8.2 2.4 %fusion.6 = f32[1,320,256]{2,1,0:T(8,128)S(1)} fusion(bf16[3456,256]{1,0:T(8,128)(2,1)} %param.12, bf16[1,320,3456]{2,1,0:T(8,128)(2,1)S(1)} %copy-done), kind=kOutput, calls=%fused_computation.10 | convolution fusion | flops 566231040 | bytes 4308992 | tf_op jit(solution)/shard_map/dot_general | solution.py:9
  10.5 0.0 copy-done.7
  10.5 0.0 copy-start.2
  10.5 0.0 copy-start.4
  10.6 0.0 copy-start.3
  10.6 5.0 %fusion.4 = f32[3,320,256]{2,1,0:T(8,128)S(1)} fusion(bf16[3,320,3456]{2,1,0:T(8,128)(2,1)} %param.8, bf16[3456,256]{1,0:T(8,128)(2,1)S(1)} %copy-done.7), kind=kOutput, calls=%fused_computation.4 | convolution fusion | flops 1698693120 | bytes 9388032 | tf_op jit(solution)/shard_map/dot_general | solution.py:9
  15.6 0.0 copy-done.2
  15.6 0.0 copy-done.4
  15.6 0.3 convolution_bitcast_fusion
  15.9 0.0 copy-done.3
  15.9 0.5 fusion.17
  16.4 1.8 pad_maximum_fusion
  18.2 0.0 all-reduce.3.cloned.1.call-update
  18.3 0.2 all-gather.3.cloned.1.call-start
  18.5 74.5 %all-reduce.3.cloned.1.call-done = (f32[4,320,256]{2,1,0:T(8,128)}, f32[4,320,256]{2,1,0:T(8,128)}) async-done(((f32[4,320,256]{2,1,0:T(8,128)}, f32[4,320,256]{2,1,0:T(8,128)}), (f32[4,320,256]{2,1,0:T(8,128)}, f32[4,320,256]{2,1,0:T(8,128)})) %all-reduce.3.cloned.1.call-update) | async-done | bytes 2621456 | tf_op jit(solution)/shard_map/psum | solution.py:31
  93.0 0.0 copy-start.5
  93.0 0.0 copy-start.6
  93.0 4.6 %convolution_multiply_fusion = f32[4,256,256]{2,1,0:T(8,128)S(1)} fusion(f32[4,320,256]{2,1,0:T(8,128)} %get-tuple-element.5, f32[4,320,256]{2,1,0:T(8,128)} %get-tuple-element.6), kind=kOutput, calls=%fused_computation.6 | convolution fusion | flops 1006895104 | bytes 3670016 | tf_op jit(solution)/shard_map/sli,slj->sij/dot_general | solution.py:34
  97.6 0.0 copy-start.1
  97.6 1.1 copy-done.1
  98.7 0.0 copy-done.5
  98.7 0.6 convolution_bitcast_fusion.1
  99.3 0.0 copy-done.6
  99.3 1.3 fusion.19
  100.6 0.0 all-gather.3.cloned.1.call-update
  100.6 1.2 slice.9
  101.8 98.4 %all-gather.3.cloned.1.call-done = f32[8192,256]{1,0:T(8,128)} async-done(((f32[256,256]{1,0:T(8,128)}), f32[8192,256]{1,0:T(8,128)}) %all-gather.3.cloned.1.call-update) | async-done | bytes 8388624 | tf_op jit(solution)/shard_map/all_gather | solution.py:41
  200.2 14.6 %fusion.12 = f32[32,3]{0,1:T(4,128)} fusion(f32[32,256,256]{2,1,0:T(8,128)} %bitcast.41, f32[3,256,256]{2,1,0:T(8,128)S(1)} %slice.9), kind=kOutput, calls=%fused_computation.13 | convolution fusion | flops 75497568 | bytes 9175424 | tf_op jit(solution)/shard_map/qij,sij->qs/dot_general | solution.py:39
Async XLA Ops:
  6.5 1.6 copy-start
  6.5 86.5 %all-reduce.3.cloned.1.call-start = ((), (), s32[]{:S(2)}) async-start(), calls=%async_computation.1 | async-start | bytes 5242880 | tf_op jit(solution)/shard_map/psum | solution.py:31
  8.2 2.4 %copy-start.7 = (bf16[3456,256]{1,0:T(8,128)(2,1)S(1)}, bf16[3456,256]{1,0:T(8,128)(2,1)}, u32[]{:S(2)}) copy-start(bf16[3456,256]{1,0:T(8,128)(2,1)} %param.12) | copy-start | bytes 5308420
  10.5 5.0 %copy-start.2 = (bf16[640,256]{1,0:T(8,128)(2,1)S(1)}, bf16[640,256]{1,0:T(8,128)(2,1)}, u32[]{:S(2)}) copy-start(bf16[640,256]{1,0:T(8,128)(2,1)} %param.13) | copy-start | bytes 983044
  10.5 5.0 %copy-start.4 = (bf16[1,320,640]{2,1,0:T(8,128)(2,1)S(1)}, bf16[1,320,640]{2,1,0:T(8,128)(2,1)}, u32[]{:S(2)}) copy-start(bf16[1,320,640]{2,1,0:T(8,128)(2,1)} %param.11) | copy-start | bytes 1228804
  10.6 5.3 %copy-start.3 = (bf16[3,320,640]{2,1,0:T(8,128)(2,1)S(1)}, bf16[3,320,640]{2,1,0:T(8,128)(2,1)}, u32[]{:S(2)}) copy-start(bf16[3,320,640]{2,1,0:T(8,128)(2,1)} %param.9) | copy-start | bytes 3686404
  18.3 181.9 %all-gather.3.cloned.1.call-start = ((), (), s32[]{:S(2)}) async-start(), calls=%async_computation | async-start | bytes 8650752 | tf_op jit(solution)/shard_map/all_gather | solution.py:41
  93.0 5.7 %copy-start.5 = (f32[256,256]{1,0:T(8,128)S(1)}, f32[256,256]{1,0:T(8,128)}, u32[]{:S(2)}) copy-start(f32[256,256]{1,0:T(8,128)} %param.14) | copy-start | bytes 786436
  93.0 6.3 %copy-start.6 = (f32[256,256]{1,0:T(8,128)S(1)}, f32[256,256]{1,0:T(8,128)}, u32[]{:S(2)}) copy-start(f32[256,256]{1,0:T(8,128)} %param.15) | copy-start | bytes 786436
  97.6 1.1 copy-start.1
Sparse Core Ops, SparseCore 0:
  18.4 74.5 all-reduce.2
  100.7 99.4 all-gather.2
where the time goes:
time: 222 us
  waiting for transfers between devices  173 us (78%)
  matrix products  29.2 us (13%)
  between operations  13.5 us (6%)
  local copies, waits for them, and re-layouts  3.9 us (2%)
    all_gather x1, waiting for transfers between devices, body(): lax.all_gather(precond, 'dp', axis=0, tiled=True)  98.4 us
    psum x1, waiting for transfers between devices, body(): lax.psum((jnp.concatenate([train_x, query_x], 0), jnp.concatenate([train_...  74.5 us
    dot_general x1, matrix products, body(): jnp.einsum('qij,sij->qs', lax.all_gather(precond, 'dp', axis=0, tiled=Tru...  14.6 us
    dot_general x4, matrix products, project(): result = jnp.dot(flat, weights, preferred_element_type=jnp.float32)  8.17 us
    dot_general x1, matrix products, body(): jnp.einsum('sli,slj->sij', out_side, in_side, precision=highest) * factor  4.57 us
  transfers between devices with their start and end apart: 2, of which 2 were waited for; matrix products, arithmetic and copies ran while one was open for 1% of the time, Pallas kernels for 0%

commit v1 on v0

v1 whole, which is shorter than its diff:
```python
import jax
import jax.numpy as jnp
from jax import lax
from jax.sharding import Mesh, PartitionSpec as P

HIGH = lax.Precision.HIGH
PAIRS_A = [(0, 1), (1, 0), (2, 3), (3, 2)]
PAIRS_B = [(0, 3), (3, 0), (1, 2), (2, 1)]
CORES = [(0, 1), (1, 0)]


def shift(value, axis, size, by):
    return lax.ppermute(value, axis, [((i + by) % size, i) for i in range(size)])


def project(acts, weights):
    return jnp.einsum("slk,kr->slr", acts, weights, preferred_element_type=jnp.float32)


def halves(value, index, axis):
    first, second = jnp.split(value, 2, axis)
    swap = index == 1
    return jnp.where(swap, second, first), jnp.where(swap, first, second)


def body(
    train_inputs,
    train_grads_out,
    query_inputs,
    query_grads_out,
    proj_in,
    proj_out,
    out_inverse,
    in_inverse,
):
    length = train_inputs.shape[1]
    width = proj_in.shape[1]
    x, z, y, core = (lax.axis_index(name) for name in ("x", "z", "y", "c"))
    row_half = ((y == 1) | (y == 2)).astype(jnp.int32)
    col_half = (y >= 2).astype(jnp.int32)

    query_y = jnp.einsum("slk,ik->sli", project(query_grads_out, proj_out), out_inverse, precision=HIGH)
    query_x = jnp.einsum("slk,kj->slj", project(query_inputs, proj_in), in_inverse, precision=HIGH)
    all_y = jnp.concatenate([query_y, project(train_grads_out, proj_out)], 0)
    all_x = jnp.concatenate([query_x, project(train_inputs, proj_in)], 0)

    keep_y, send_y = halves(all_y, core, 0)
    keep_x, send_x = halves(all_x, core, 0)
    sum_y = keep_y + lax.ppermute(send_y, "c", CORES)
    sum_x = keep_x + lax.ppermute(send_x, "c", CORES)

    keep_y, send_y = halves(sum_y, row_half, 2)
    keep_x, send_x = halves(sum_x, col_half, 2)
    half_y = keep_y + lax.ppermute(send_y, "y", PAIRS_A)
    half_x = keep_x + lax.ppermute(send_x, "y", PAIRS_B)
    half_y = half_y + lax.ppermute(half_y, "y", PAIRS_B)
    half_x = half_x + lax.ppermute(half_x, "y", PAIRS_A)

    grads = jnp.einsum("sli,slj->sij", half_y, half_x, precision=HIGH)
    keep, send = halves(grads, core, 1)
    got = lax.ppermute(send, "c", CORES)
    low = jnp.where(core == 0, keep, got)
    high = jnp.where(core == 0, got, keep)
    query, train = low[:1], jnp.concatenate([low[1:], high], 0)

    near = jnp.concatenate([query, shift(query, "z", 8, 1), shift(query, "z", 8, -1)], 0)
    up = shift(near, "z", 8, 3)
    down = shift(near[:2], "z", 8, -3)
    queries = jnp.concatenate([near, up, down], 0)
    at_z = [0, 1, -1, 3, 4, 2, -3, -2]
    trains = jnp.stack([train] + [shift(train, "x", 4, by) for by in (1, 2, 3)], 0)
    part = jnp.einsum("qij,dsij->qds", queries, trains, precision=lax.Precision.HIGHEST)

    part = jnp.stack([part[:, (i - x) % 4] for i in range(4)], 0)
    part = jnp.broadcast_to(part[:, None], (4, 8) + part.shape[1:]).reshape((32,) + part.shape[1:])
    got = lax.all_to_all(part, ("x", "y", "c"), 0, 0, tiled=True)
    scores = got.reshape(4, 8, 8, 3).sum(1)
    order = [at_z.index(d) if d in at_z else at_z.index(d - 8) for d in range(8)]
    scores = scores[:, jnp.array(order)]
    scores = jnp.roll(scores, z, 1)
    return scores.reshape(32, 3) * (1.0 / (length * width))


def solution(mesh):
    devices = Mesh(mesh.devices.reshape(4, 8, 4, 2), ("x", "z", "y", "c"))
    dp, mp = ("x", "z"), ("y", "c")
    return jax.shard_map(
        body,
        mesh=devices,
        in_specs=(
            P(dp, None, mp),
            P(dp, None, mp),
            P(dp, None, mp),
            P(dp, None, mp),
            P(mp, None),
            P(mp, None),
            P(),
            P(),
        ),
        out_specs=P(None, dp),
        check_vma=False,
    )
```

time: 222 us -> 79.1 us (0.36)
  waiting for transfers between devices: 173 us -> 27.9 us
  starting transfers between devices: 0.22 us -> 30.3 us
  matrix products: 29.2 us -> 12.1 us
  between operations: 13.5 us -> 0.33 us
  other arithmetic: 1.79 us -> 4.87 us
    all_gather x1 -> x0, waiting for transfers between devices: 98.4 us -> none  [body(): lax.all_gather(precond, 'dp', axis=0, tiled=True)]
    psum x1 -> x0, waiting for transfers between devices: 74.5 us -> none  [body(): lax.psum((jnp.concatenate([train_x, query_x], 0), jnp.concatenate([train_...]
    ppermute x0 -> x14, waiting for transfers between devices: none -> 20.6 us  [the longest x1 5.91 us: body(): half_y = half_y + lax.ppermute(half_y, 'y', PAIRS_B)]
    ppermute x0 -> x14, starting transfers between devices: none -> 20.6 us  [the longest x7 12.7 us: shift(): lax.ppermute(value, axis, [((i + by) % size, i) for i in range(size)])]
    dot_general x8, matrix products: 29.2 us -> 12.1 us  [the longest x4 8.69 us: project(): jnp.einsum('slk,kr->slr', acts, weights, preferred_element_type=jnp.float32)]
    all_to_all x0 -> x1, starting transfers between devices: none -> 9.77 us  [body(): got = lax.all_to_all(part, ('x', 'y', 'c'), 0, 0, tiled=True)]
    all_to_all x0 -> x1, waiting for transfers between devices: none -> 7.33 us  [body(): got = lax.all_to_all(part, ('x', 'y', 'c'), 0, 0, tiled=True)]
    add x0 -> x4, other arithmetic: none -> 2.71 us  [the longest x1 1.38 us: body(): sum_y = keep_y + lax.ppermute(send_y, 'c', CORES)]
  transfers between devices with their start and end apart: 2 -> 15, of which waited for: 2 -> 8; matrix products, arithmetic and copies ran while one was open for 1% -> 12% of each run, Pallas kernels for 0% -> 0%
where the time goes in v1:
time: 79.1 us; the launch traced here: 78.1 us
  starting transfers between devices  30.3 us (38%)
  waiting for transfers between devices  27.9 us (35%)
  matrix products  12.1 us (15%)
  other arithmetic  4.87 us (6%)
  local copies, waits for them, and re-layouts  2.53 us (3%)
    ppermute x7, starting transfers between devices, shift(): lax.ppermute(value, axis, [((i + by) % size, i) for i in range(size)])  12.7 us
    all_to_all x1, starting transfers between devices, body(): got = lax.all_to_all(part, ('x', 'y', 'c'), 0, 0, tiled=True)  9.77 us
    dot_general x4, matrix products, project(): jnp.einsum('slk,kr->slr', acts, weights, preferred_element_type=jnp.float32)  8.69 us
    all_to_all x1, waiting for transfers between devices, body(): got = lax.all_to_all(part, ('x', 'y', 'c'), 0, 0, tiled=True)  7.33 us
    ppermute x1, waiting for transfers between devices, body(): half_y = half_y + lax.ppermute(half_y, 'y', PAIRS_B)  5.91 us
    ppermute x1, waiting for transfers between devices, body(): half_y = keep_y + lax.ppermute(send_y, 'y', PAIRS_A)  5.5 us
    ppermute x1, starting transfers between devices, body(): sum_y = keep_y + lax.ppermute(send_y, 'c', CORES)  3.24 us
    ppermute x1, waiting for transfers between devices, body(): half_x = keep_x + lax.ppermute(send_x, 'y', PAIRS_B)  2.74 us
  transfers between devices with their start and end apart: 15, of which 8 were waited for; matrix products, arithmetic and copies ran while one was open for 12% of the time, Pallas kernels for 0%

profile of v1, /device:TPU:1, one launch (start us, length us, event | category | flops | bytes accessed | tf_op | source)
XLA Modules:
  0.0 78.1 jit_solution(16841219591347710618)
XLA Ops:
  0.0 2.0 %fusion.7 = f32[3,320,256]{2,1,0:T(8,128)S(1)} fusion(bf16[3,320,640]{2,1,0:T(8,128)(2,1)} %param.10, bf16[640,256]{1,0:T(8,128)(2,1)} %param.14), kind=kOutput, calls=%fused_computation.18 | convolution fusion | flops 314572800 | bytes 2539520 | tf_op jit(solution)/shard_map/slk,kr->slr/dot_general | solution.py:17
  2.1 1.0 %fusion.4 = f32[320,256]{1,0:T(8,128)} fusion(bf16[640,256]{1,0:T(8,128)(2,1)S(1)} %copy-done.4, bf16[1,320,640]{2,1,0:T(8,128)(2,1)S(1)} %copy-done.5), kind=kOutput, calls=%fused_computation.14 | convolution fusion | flops 104857600 | bytes 1064960 | tf_op jit(solution)/shard_map/slk,kr->slr/dot_general | solution.py:17
  3.1 1.5 %convolution_bitcast_fusion.1 = f32[1,320,256]{2,1,0:T(8,128)S(1)} fusion(f32[320,256]{1,0:T(8,128)} %fusion.4, f32[256,256]{1,0:T(8,128)} %param.15), kind=kOutput, calls=%fused_computation.6 | convolution fusion | flops 125829120 | bytes 917504 | tf_op jit(solution)/shard_map/slk,ik->sli/dot_general | solution.py:42
  4.7 0.9 %slice_select_fusion.1 = f32[2,320,256]{2,1,0:T(8,128)} fusion(f32[3,320,256]{2,1,0:T(8,128)S(1)} %fusion.7, pred[]{:T(512)S(6)} %eq.30, f32[1,320,256]{2,1,0:T(8,128)S(1)} %convolution_bitcast_fusion.1), kind=kLoop, calls=%fused_computation.13 | loop fusion | flops 327680 | bytes 2621441 | tf_op jit(solution)/shard_map/jit(_where)/select_n | solution.py:23
  5.6 3.2 %collective-permute-start = (f32[2,320,256]{2,1,0:T(8,128)}, f32[2,320,256]{2,1,0:T(8,128)}, u32[]{:S(2)}, u32[]{:S(2)}) collective-permute-start(f32[2,320,256]{2,1,0:T(8,128)} %slice_select_fusion.1), channel_id=1, source_target_pairs={{0,1},{1,0},{2,3},{3,2},{4,5},{5,4},{6,7},{7,6},{8,9},{9,8},{10,11... | collective-permute-start | bytes 1966088 | tf_op jit(solution)/shard_map/ppermute | solution.py:49
  8.8 4.8 %fusion.2 = f32[3,320,256]{2,1,0:T(8,128)S(1)} fusion(bf16[3,320,3456]{2,1,0:T(8,128)(2,1)} %param.9, bf16[3456,256]{1,0:T(8,128)(2,1)S(1)} %copy-done.8), kind=kOutput, calls=%fused_computation.3 | convolution fusion | flops 1698693120 | bytes 9388032 | tf_op jit(solution)/shard_map/slk,kr->slr/dot_general | solution.py:17
  13.7 0.8 %fusion = f32[320,256]{1,0:T(8,128)S(1)} fusion(bf16[3456,256]{1,0:T(8,128)(2,1)S(1)} %copy-done.8, bf16[1,320,3456]{2,1,0:T(8,128)(2,1)S(1)} %copy-done), kind=kOutput, calls=%fused_computation.1 | convolution fusion | flops 566231040 | bytes 4308992 | tf_op jit(solution)/shard_map/slk,kr->slr/dot_general | solution.py:17
  15.2 0.9 %slice_select_fusion = f32[2,320,256]{2,1,0:T(8,128)} fusion(f32[3,320,256]{2,1,0:T(8,128)S(1)} %fusion.2, pred[]{:T(512)S(6)} %eq.30, f32[1,320,256]{2,1,0:T(8,128)S(1)} %convolution_bitcast_fusion), kind=kLoop, calls=%fused_computation.12 | loop fusion | flops 327680 | bytes 2621441 | tf_op jit(solution)/shard_map/jit(_where)/select_n | solution.py:23
  16.1 1.4 %select_add_fusion.1 = f32[2,320,256]{2,1,0:T(8,128)S(1)} fusion(f32[2,320,256]{2,1,0:T(8,128)} %collective-permute-done, f32[3,320,256]{2,1,0:T(8,128)S(1)} %fusion.7, pred[]{:T(512)S(6)} %eq.30, f32[1,320,256]{2,1,0:T(8,128)} %copy-done.3), kind=kLoop, calls=%fused_computation.11 | loop fusion | flops 491520 | bytes 3276801 | tf_op jit(solution)/shard_map/add | solution.py:49
  17.7 0.9 %collective-permute-done.3 = f32[2,320,256]{2,1,0:T(8,128)} collective-permute-done((f32[2,320,256]{2,1,0:T(8,128)}, f32[2,320,256]{2,1,0:T(8,128)}, u32[]{:S(2)}, u32[]{:S(2)}) %collective-permute-start.3) | collective-permute-done | bytes 655392 | tf_op jit(solution)/shard_map/ppermute | solution.py:50
  18.6 1.2 %select_add_fusion = f32[2,320,256]{2,1,0:T(8,128)S(1)} fusion(f32[2,320,256]{2,1,0:T(8,128)} %collective-permute-done.3, f32[3,320,256]{2,1,0:T(8,128)S(1)} %copy-done.2, pred[]{:T(512)S(6)} %eq.30, f32[1,320,256]{2,1,0:T(8,128)S(1)} %convolution_bitcast_fusion), kind=kLoop, calls=%fused_computation.10 | loop fusion | flops 491520 | bytes 3276801 | tf_op jit(solution)/shard_map/add | solution.py:50
  19.8 1.1 %collective-permute-start.4 = (f32[2,320,128]{2,1,0:T(8,128)S(1)}, f32[2,320,128]{2,1,0:T(8,128)S(1)}, u32[]{:S(2)}, u32[]{:S(2)}) collective-permute-start(f32[2,320,128]{2,1,0:T(8,128)S(1)} %slice_select_fusion.2), channel_id=1, source_target_pairs={{0,6},{6,0},{2,4},{4,2},{1,7},{7,1},{3,5},{5,3},{8,14},{14,8},{10,... | collective-permute-start | bytes 983048 | tf_op jit(solution)/shard_map/ppermute | solution.py:55
  20.9 5.5 %collective-permute-done.1 = f32[2,320,128]{2,1,0:T(8,128)S(1)} collective-permute-done((f32[2,320,128]{2,1,0:T(8,128)S(1)}, f32[2,320,128]{2,1,0:T(8,128)S(1)}, u32[]{:S(2)}, u32[]{:S(2)}) %collective-permute-start.1) | collective-permute-done | bytes 327712 | tf_op jit(solution)/shard_map/ppermute | solution.py:54
  26.5 1.1 %collective-permute-start.2 = (f32[2,320,128]{2,1,0:T(8,128)S(1)}, f32[2,320,128]{2,1,0:T(8,128)S(1)}, u32[]{:S(2)}, u32[]{:S(2)}) collective-permute-start(f32[2,320,128]{2,1,0:T(8,128)S(1)} %select_add_fusion.3), channel_id=1, source_target_pairs={{0,6},{6,0},{2,4},{4,2},{1,7},{7,1},{3,5},{5,3},{8,14},{14,8},{10,... | collective-permute-start | bytes 983048 | tf_op jit(solution)/shard_map/ppermute | solution.py:56
  27.5 2.7 %collective-permute-done.4 = f32[2,320,128]{2,1,0:T(8,128)S(1)} collective-permute-done((f32[2,320,128]{2,1,0:T(8,128)S(1)}, f32[2,320,128]{2,1,0:T(8,128)S(1)}, u32[]{:S(2)}, u32[]{:S(2)}) %collective-permute-start.4) | collective-permute-done | bytes 327712 | tf_op jit(solution)/shard_map/ppermute | solution.py:55
  30.4 5.9 %collective-permute-done.2 = f32[2,320,128]{2,1,0:T(8,128)S(1)} collective-permute-done((f32[2,320,128]{2,1,0:T(8,128)S(1)}, f32[2,320,128]{2,1,0:T(8,128)S(1)}, u32[]{:S(2)}, u32[]{:S(2)}) %collective-permute-start.2) | collective-permute-done | bytes 327712 | tf_op jit(solution)/shard_map/ppermute | solution.py:56
  36.4 2.0 %collective-permute-done.5 = f32[2,320,128]{2,1,0:T(8,128)S(1)} collective-permute-done((f32[2,320,128]{2,1,0:T(8,128)S(1)}, f32[2,320,128]{2,1,0:T(8,128)S(1)}, u32[]{:S(2)}, u32[]{:S(2)}) %collective-permute-start.5) | collective-permute-done | bytes 327712 | tf_op jit(solution)/shard_map/ppermute | solution.py:57
  38.9 2.3 %collective-permute-start.6 = (f32[2,64,128]{2,1,0:T(8,128)S(1)}, f32[2,64,128]{2,1,0:T(8,128)S(1)}, u32[]{:S(2)}, u32[]{:S(2)}) collective-permute-start(f32[2,64,128]{2,1,0:T(8,128)S(1)} %slice_select_fusion.4), channel_id=1, source_target_pairs={{0,1},{1,0},{2,3},{3,2},{4,5},{5,4},{6,7},{7,6},{8,9},{9,8},{10,11... | collective-permute-start | bytes 196616 | tf_op jit(solution)/shard_map/ppermute | solution.py:61
  41.2 0.9 %collective-permute-done.6 = f32[2,64,128]{2,1,0:T(8,128)S(1)} collective-permute-done((f32[2,64,128]{2,1,0:T(8,128)S(1)}, f32[2,64,128]{2,1,0:T(8,128)S(1)}, u32[]{:S(2)}, u32[]{:S(2)}) %collective-permute-start.6) | collective-permute-done | bytes 65568 | tf_op jit(solution)/shard_map/ppermute | solution.py:61
  42.1 3.6 %collective-permute-start.7 = (f32[1,64,128]{2,1,0:T(8,128)S(1)}, f32[1,64,128]{2,1,0:T(8,128)S(1)}, u32[]{:S(2)}, u32[]{:S(2)}) collective-permute-start(f32[1,64,128]{2,1,0:T(8,128)S(1)} %get-tuple-element.9), channel_id=1, source_target_pairs={{8,0},{16,8},{24,16},{32,24},{40,32},{48,40},{56,48},{0,56},{9,1},... | collective-permute-start | bytes 98312 | tf_op jit(solution)/shard_map/ppermute | solution.py:13
  45.7 1.3 %collective-permute-start.13 = (f32[3,64,128]{2,1,0:T(8,128)S(1)}, f32[3,64,128]{2,1,0:T(8,128)S(1)}, u32[]{:S(2)}, u32[]{:S(2)}) collective-permute-start(f32[3,64,128]{2,1,0:T(8,128)S(1)} %get-tuple-element.8), channel_id=1, source_target_pairs={{192,0},{0,64},{64,128},{128,192},{193,1},{1,65},{65,129},{129,193... | collective-permute-start | bytes 294920 | tf_op jit(solution)/shard_map/ppermute | solution.py:13
  47.0 1.5 %collective-permute-start.11 = (f32[3,64,128]{2,1,0:T(8,128)S(1)}, f32[3,64,128]{2,1,0:T(8,128)S(1)}, u32[]{:S(2)}, u32[]{:S(2)}) collective-permute-start(f32[3,64,128]{2,1,0:T(8,128)S(1)} %get-tuple-element.8), channel_id=1, source_target_pairs={{64,0},{128,64},{192,128},{0,192},{65,1},{129,65},{193,129},{1,193... | collective-permute-start | bytes 294920 | tf_op jit(solution)/shard_map/ppermute | solution.py:13
  48.5 1.5 %collective-permute-start.12 = (f32[3,64,128]{2,1,0:T(8,128)S(1)}, f32[3,64,128]{2,1,0:T(8,128)S(1)}, u32[]{:S(2)}, u32[]{:S(2)}) collective-permute-start(f32[3,64,128]{2,1,0:T(8,128)S(1)} %get-tuple-element.8), channel_id=1, source_target_pairs={{128,0},{192,64},{0,128},{64,192},{129,1},{193,65},{1,129},{65,193... | collective-permute-start | bytes 294920 | tf_op jit(solution)/shard_map/ppermute | solution.py:13
  50.0 2.0 %collective-permute-start.10 = (f32[2,64,128]{2,1,0:T(8,128)S(1)}, f32[2,64,128]{2,1,0:T(8,128)S(1)}, u32[]{:S(2)}, u32[]{:S(2)}) collective-permute-start(f32[2,64,128]{2,1,0:T(8,128)S(1)} %pad_maximum_fusion.5), channel_id=1, source_target_pairs={{40,0},{48,8},{56,16},{0,24},{8,32},{16,40},{24,48},{32,56},{41,1}... | collective-permute-start | bytes 196616 | tf_op jit(solution)/shard_map/ppermute | solution.py:13
  52.0 2.8 %collective-permute-start.9 = (f32[3,64,128]{2,1,0:T(8,128)S(1)}, f32[3,64,128]{2,1,0:T(8,128)S(1)}, u32[]{:S(2)}, u32[]{:S(2)}) collective-permute-start(f32[3,64,128]{2,1,0:T(8,128)S(1)} %pad_maximum_fusion.3), channel_id=1, source_target_pairs={{24,0},{32,8},{40,16},{48,24},{56,32},{0,40},{8,48},{16,56},{25,1}... | collective-permute-start | bytes 294920 | tf_op jit(solution)/shard_map/ppermute | solution.py:13
  54.9 2.6 %collective-permute-done.9 = f32[3,64,128]{2,1,0:T(8,128)S(1)} collective-permute-done((f32[3,64,128]{2,1,0:T(8,128)S(1)}, f32[3,64,128]{2,1,0:T(8,128)S(1)}, u32[]{:S(2)}, u32[]{:S(2)}) %collective-permute-start.9) | collective-permute-done | bytes 98336 | tf_op jit(solution)/shard_map/ppermute | solution.py:13
  57.6 1.1 %convolution_bitcast_fusion.2 = f32[8,4,3]{0,1,2:T(4,128)S(1)} fusion(f32[4,3,64,128]{3,2,1,0:T(8,128)S(1)} %pad_maximum_fusion.2, f32[8,64,128]{2,1,0:T(8,128)S(1)} %constant_dynamic-update-slice_fusion), kind=kOutput, calls=%fused_computation.7 | convolution fusion | flops 9437184 | bytes 655744 | tf_op jit(solution)/shard_map/qij,dsij->qds/dot_general | solution.py:72
  58.8 0.6 broadcast_in_dim.4
  59.4 9.8 %all-to-all-start = ((f32[32,8,3]{1,2,0:T(4,128)}), f32[32,8,3]{1,2,0:T(4,128)S(1)}, u32[]{:S(2)}, u32[]{:S(2)}) async-start(f32[32,8,3]{1,2,0:T(4,128)} %bitcast.17), calls=%async_computation | async-start | bytes 131072 | tf_op jit(solution)/shard_map/all_to_all | solution.py:76
  69.2 7.3 %all-to-all-done = f32[32,8,3]{1,2,0:T(4,128)S(1)} async-done(((f32[32,8,3]{1,2,0:T(4,128)}), f32[32,8,3]{1,2,0:T(4,128)S(1)}, u32[]{:S(2)}, u32[]{:S(2)}) %all-to-all-start) | async-done | bytes 3104 | tf_op jit(solution)/shard_map/all_to_all | solution.py:76
  76.7 0.6 gather_fusion
  77.4 0.7 mul.11
  (54 shorter events, 2.0 us)
Async XLA Ops:
  0.0 13.7 %copy-start = (bf16[1,320,3456]{2,1,0:T(8,128)(2,1)S(1)}, bf16[1,320,3456]{2,1,0:T(8,128)(2,1)}, u32[]{:S(2)}) copy-start(bf16[1,320,3456]{2,1,0:T(8,128)(2,1)} %param.11) | copy-start | bytes 6635524
  0.0 2.1 %copy-start.4 = (bf16[640,256]{1,0:T(8,128)(2,1)S(1)}, bf16[640,256]{1,0:T(8,128)(2,1)}, u32[]{:S(2)}) copy-start(bf16[640,256]{1,0:T(8,128)(2,1)} %param.14) | copy-start | bytes 983044
  0.0 2.1 %copy-start.5 = (bf16[1,320,640]{2,1,0:T(8,128)(2,1)S(1)}, bf16[1,320,640]{2,1,0:T(8,128)(2,1)}, u32[]{:S(2)}) copy-start(bf16[1,320,640]{2,1,0:T(8,128)(2,1)} %param.12) | copy-start | bytes 1228804
  3.1 5.7 %copy-start.8 = (bf16[3456,256]{1,0:T(8,128)(2,1)S(1)}, bf16[3456,256]{1,0:T(8,128)(2,1)}, u32[]{:S(2)}) copy-start(bf16[3456,256]{1,0:T(8,128)(2,1)} %param.13) | copy-start | bytes 5308420
  4.6 1.0 %copy-start.3 = (f32[1,320,256]{2,1,0:T(8,128)}, f32[1,320,256]{2,1,0:T(8,128)S(1)}, u32[]{:S(2)}) copy-start(f32[1,320,256]{2,1,0:T(8,128)S(1)} %convolution_bitcast_fusion.1) | copy-start | bytes 983044
  5.6 10.5 %collective-permute-start = (f32[2,320,256]{2,1,0:T(8,128)}, f32[2,320,256]{2,1,0:T(8,128)}, u32[]{:S(2)}, u32[]{:S(2)}) collective-permute-start(f32[2,320,256]{2,1,0:T(8,128)} %slice_select_fusion.1), channel_id=1, source_target_pairs={{0,1},{1,0},{2,3},{3,2},{4,5},{5,4},{6,7},{7,6},{8,9},{9,8},{10,11... | collective-permute-start | bytes 1966088 | tf_op jit(solution)/shard_map/ppermute | solution.py:49
  13.7 1.5 %copy-start.1 = (f32[3,320,256]{2,1,0:T(8,128)}, f32[3,320,256]{2,1,0:T(8,128)S(1)}, u32[]{:S(2)}) copy-start(f32[3,320,256]{2,1,0:T(8,128)S(1)} %fusion.2) | copy-start | bytes 2949124
  13.7 1.1 %copy-start.6 = (f32[256,256]{1,0:T(8,128)S(1)}, f32[256,256]{1,0:T(8,128)}, u32[]{:S(2)}) copy-start(f32[256,256]{1,0:T(8,128)} %param.16) | copy-start | bytes 786436
  16.1 2.4 %collective-permute-start.3 = (f32[2,320,256]{2,1,0:T(8,128)}, f32[2,320,256]{2,1,0:T(8,128)}, u32[]{:S(2)}, u32[]{:S(2)}) collective-permute-start(f32[2,320,256]{2,1,0:T(8,128)} %slice_select_fusion), channel_id=1, source_target_pairs={{0,1},{1,0},{2,3},{3,2},{4,5},{5,4},{6,7},{7,6},{8,9},{9,8},{10,11... | collective-permute-start | bytes 1966088 | tf_op jit(solution)/shard_map/ppermute | solution.py:50
  16.1 2.4 %copy-start.2 = (f32[3,320,256]{2,1,0:T(8,128)S(1)}, f32[3,320,256]{2,1,0:T(8,128)}, u32[]{:S(2)}) copy-start(f32[3,320,256]{2,1,0:T(8,128)} %copy-done.1) | copy-start | bytes 2949124
  17.6 8.9 %collective-permute-start.1 = (f32[2,320,128]{2,1,0:T(8,128)S(1)}, f32[2,320,128]{2,1,0:T(8,128)S(1)}, u32[]{:S(2)}, u32[]{:S(2)}) collective-permute-start(f32[2,320,128]{2,1,0:T(8,128)S(1)} %slice_select_fusion.3), channel_id=1, source_target_pairs={{0,2},{2,0},{4,6},{6,4},{1,3},{3,1},{5,7},{7,5},{8,10},{10,8},{12,... | collective-permute-start | bytes 983048 | tf_op jit(solution)/shard_map/ppermute | solution.py:54
  19.8 10.5 %collective-permute-start.4 = (f32[2,320,128]{2,1,0:T(8,128)S(1)}, f32[2,320,128]{2,1,0:T(8,128)S(1)}, u32[]{:S(2)}, u32[]{:S(2)}) collective-permute-start(f32[2,320,128]{2,1,0:T(8,128)S(1)} %slice_select_fusion.2), channel_id=1, source_target_pairs={{0,6},{6,0},{2,4},{4,2},{1,7},{7,1},{3,5},{5,3},{8,14},{14,8},{10,... | collective-permute-start | bytes 983048 | tf_op jit(solution)/shard_map/ppermute | solution.py:55
  26.5 9.9 %collective-permute-start.2 = (f32[2,320,128]{2,1,0:T(8,128)S(1)}, f32[2,320,128]{2,1,0:T(8,128)S(1)}, u32[]{:S(2)}, u32[]{:S(2)}) collective-permute-start(f32[2,320,128]{2,1,0:T(8,128)S(1)} %select_add_fusion.3), channel_id=1, source_target_pairs={{0,6},{6,0},{2,4},{4,2},{1,7},{7,1},{3,5},{5,3},{8,14},{14,8},{10,... | collective-permute-start | bytes 983048 | tf_op jit(solution)/shard_map/ppermute | solution.py:56
  30.3 8.0 %collective-permute-start.5 = (f32[2,320,128]{2,1,0:T(8,128)S(1)}, f32[2,320,128]{2,1,0:T(8,128)S(1)}, u32[]{:S(2)}, u32[]{:S(2)}) collective-permute-start(f32[2,320,128]{2,1,0:T(8,128)S(1)} %select_add_fusion.2), channel_id=1, source_target_pairs={{0,2},{2,0},{4,6},{6,4},{1,3},{3,1},{5,7},{7,5},{8,10},{10,8},{12,... | collective-permute-start | bytes 983048 | tf_op jit(solution)/shard_map/ppermute | solution.py:57
  38.9 30.3 %copy-start.7 = (s32[8]{0:T(128)S(1)}, s32[8]{0:T(128)}, u32[]{:S(2)}) copy-start(s32[8]{0:T(128)} %constant.85) | copy-start | bytes 100
  38.9 3.2 %collective-permute-start.6 = (f32[2,64,128]{2,1,0:T(8,128)S(1)}, f32[2,64,128]{2,1,0:T(8,128)S(1)}, u32[]{:S(2)}, u32[]{:S(2)}) collective-permute-start(f32[2,64,128]{2,1,0:T(8,128)S(1)} %slice_select_fusion.4), channel_id=1, source_target_pairs={{0,1},{1,0},{2,3},{3,2},{4,5},{5,4},{6,7},{7,6},{8,9},{9,8},{10,11... | collective-permute-start | bytes 196616 | tf_op jit(solution)/shard_map/ppermute | solution.py:61
  42.1 7.9 %collective-permute-start.7 = (f32[1,64,128]{2,1,0:T(8,128)S(1)}, f32[1,64,128]{2,1,0:T(8,128)S(1)}, u32[]{:S(2)}, u32[]{:S(2)}) collective-permute-start(f32[1,64,128]{2,1,0:T(8,128)S(1)} %get-tuple-element.9), channel_id=1, source_target_pairs={{8,0},{16,8},{24,16},{32,24},{40,32},{48,40},{56,48},{0,56},{9,1},... | collective-permute-start | bytes 98312 | tf_op jit(solution)/shard_map/ppermute | solution.py:13
  45.7 6.3 %collective-permute-start.8 = (f32[1,64,128]{2,1,0:T(8,128)S(1)}, f32[1,64,128]{2,1,0:T(8,128)S(1)}, u32[]{:S(2)}, u32[]{:S(2)}) collective-permute-start(f32[1,64,128]{2,1,0:T(8,128)S(1)} %get-tuple-element.9), channel_id=1, source_target_pairs={{56,0},{0,8},{8,16},{16,24},{24,32},{32,40},{40,48},{48,56},{57,1}... | collective-permute-start | bytes 98312 | tf_op jit(solution)/shard_map/ppermute | solution.py:13
  45.7 9.1 %collective-permute-start.13 = (f32[3,64,128]{2,1,0:T(8,128)S(1)}, f32[3,64,128]{2,1,0:T(8,128)S(1)}, u32[]{:S(2)}, u32[]{:S(2)}) collective-permute-start(f32[3,64,128]{2,1,0:T(8,128)S(1)} %get-tuple-element.8), channel_id=1, source_target_pairs={{192,0},{0,64},{64,128},{128,192},{193,1},{1,65},{65,129},{129,193... | collective-permute-start | bytes 294920 | tf_op jit(solution)/shard_map/ppermute | solution.py:13
  47.0 7.9 %collective-permute-start.11 = (f32[3,64,128]{2,1,0:T(8,128)S(1)}, f32[3,64,128]{2,1,0:T(8,128)S(1)}, u32[]{:S(2)}, u32[]{:S(2)}) collective-permute-start(f32[3,64,128]{2,1,0:T(8,128)S(1)} %get-tuple-element.8), channel_id=1, source_target_pairs={{64,0},{128,64},{192,128},{0,192},{65,1},{129,65},{193,129},{1,193... | collective-permute-start | bytes 294920 | tf_op jit(solution)/shard_map/ppermute | solution.py:13
  48.5 6.4 %collective-permute-start.12 = (f32[3,64,128]{2,1,0:T(8,128)S(1)}, f32[3,64,128]{2,1,0:T(8,128)S(1)}, u32[]{:S(2)}, u32[]{:S(2)}) collective-permute-start(f32[3,64,128]{2,1,0:T(8,128)S(1)} %get-tuple-element.8), channel_id=1, source_target_pairs={{128,0},{192,64},{0,128},{64,192},{129,1},{193,65},{1,129},{65,193... | collective-permute-start | bytes 294920 | tf_op jit(solution)/shard_map/ppermute | solution.py:13
  50.0 7.5 %collective-permute-start.10 = (f32[2,64,128]{2,1,0:T(8,128)S(1)}, f32[2,64,128]{2,1,0:T(8,128)S(1)}, u32[]{:S(2)}, u32[]{:S(2)}) collective-permute-start(f32[2,64,128]{2,1,0:T(8,128)S(1)} %pad_maximum_fusion.5), channel_id=1, source_target_pairs={{40,0},{48,8},{56,16},{0,24},{8,32},{16,40},{24,48},{32,56},{41,1}... | collective-permute-start | bytes 196616 | tf_op jit(solution)/shard_map/ppermute | solution.py:13
  52.0 5.5 %collective-permute-start.9 = (f32[3,64,128]{2,1,0:T(8,128)S(1)}, f32[3,64,128]{2,1,0:T(8,128)S(1)}, u32[]{:S(2)}, u32[]{:S(2)}) collective-permute-start(f32[3,64,128]{2,1,0:T(8,128)S(1)} %pad_maximum_fusion.3), channel_id=1, source_target_pairs={{24,0},{32,8},{40,16},{48,24},{56,32},{0,40},{8,48},{16,56},{25,1}... | collective-permute-start | bytes 294920 | tf_op jit(solution)/shard_map/ppermute | solution.py:13
  59.4 17.1 %all-to-all-start = ((f32[32,8,3]{1,2,0:T(4,128)}), f32[32,8,3]{1,2,0:T(4,128)S(1)}, u32[]{:S(2)}, u32[]{:S(2)}) async-start(f32[32,8,3]{1,2,0:T(4,128)} %bitcast.17), calls=%async_computation | async-start | bytes 131072 | tf_op jit(solution)/shard_map/all_to_all | solution.py:76

commit v2 on v1

v2 whole, which is shorter than its diff:
```python
import functools

import jax
import jax.numpy as jnp
from jax import lax
from jax.experimental import pallas as pl
from jax.experimental.pallas import tpu as pltpu
from jax.sharding import Mesh, PartitionSpec as P

PAIRS_A = [(0, 1), (1, 0), (2, 3), (3, 2)]
PAIRS_B = [(0, 3), (3, 0), (1, 2), (2, 1)]
CORES = [(0, 1), (1, 0)]
HALF = 128
LIMIT = 24 * 2**20
WIDE = 58 * 2**20
AT_Z = (0, 7, 2, 5, 1, 6, 3, 4)


def across(value, axis, bits):
    size = {"x": 4, "z": 8}[axis]
    return lax.ppermute(value, axis, [(i, i ^ bits) for i in range(size)])


def after(value, *others):
    return lax.optimization_barrier((value, others))[0]


def dot3(a, b, dims):
    a_high, b_high = a.astype(jnp.bfloat16), b.astype(jnp.bfloat16)
    a_low = (a - a_high.astype(jnp.float32)).astype(jnp.bfloat16)
    b_low = (b - b_high.astype(jnp.float32)).astype(jnp.bfloat16)
    dot = functools.partial(
        lax.dot_general, dimension_numbers=(dims, ((), ())), preferred_element_type=jnp.float32
    )
    return dot(a_low, b_high) + dot(a_high, b_low) + dot(a_high, b_high)


def my_halves():
    y = lax.axis_index("y")
    return jnp.where((y == 1) | (y == 2), 1, 0), jnp.where(y >= 2, 1, 0)


def project_kernel(*refs):
    (tx, ty, qx, qy, w, v, oi, ii), refs = refs[:8], refs[8:]
    (q_keep, q_send, t_keep, t_send), refs = refs[:4], refs[4:]
    x_s, y_s, w_s, v_s, oi_s, ii_s, x_acc, y_acc, sems = refs
    n, length = tx.shape[:2]
    rows = [pl.ds(s * length, length) for s in range(n + 1)]
    for_y = [(v, v_s), (oi, oi_s), (qy.at[0], y_s.at[rows[0]])]
    for_y += [(ty.at[s], y_s.at[rows[s + 1]]) for s in range(n)]
    for_x = [(w, w_s), (ii, ii_s), (qx.at[0], x_s.at[rows[0]])]
    for_x += [(tx.at[s], x_s.at[rows[s + 1]]) for s in range(n)]
    copies = [pltpu.make_async_copy(a, b, sems.at[i]) for i, (a, b) in enumerate(for_y + for_x)]
    for copy in copies:
        copy.start()
    query = pl.ds(0, length)
    for copy in copies[: len(for_y)]:
        copy.wait()
    y_acc[...] = jnp.dot(y_s[...], v_s[...], preferred_element_type=jnp.float32)
    y_acc[query] = dot3(y_acc[query], oi_s[...], ((1,), (1,)))
    for copy in copies[len(for_y) :]:
        copy.wait()
    x_acc[...] = jnp.dot(x_s[...], w_s[...], preferred_element_type=jnp.float32)
    x_acc[query] = dot3(x_acc[query], ii_s[...], ((1,), (0,)))
    part = length // 2
    core = lax.axis_index("c")
    for kind, (acc, half) in enumerate(zip((y_acc, x_acc), my_halves())):
        for j in range(2):
            place = kind + 2 * jnp.where(half == j, 1, 0)
            columns = slice(j * HALF, (j + 1) * HALF)
            for s in range(n + 1):
                keep, send, t = (q_keep, q_send, 0) if s == 0 else (t_keep, t_send, s - 1)
                mine = pl.multiple_of(s * length + core * part, part)
                other = pl.multiple_of(s * length + (1 - core) * part, part)
                keep[place, t] = acc[pl.ds(mine, part), columns]
                send[place, t] = acc[pl.ds(other, part), columns]


def project(*args):
    n, length, depth = args[0].shape
    tokens, width = (n + 1) * length, args[4].shape[1]
    outs = [jax.ShapeDtypeStruct((4, k, length // 2, HALF), jnp.float32) for k in (1, 1, n, n)]
    return pl.pallas_call(
        project_kernel,
        in_specs=[pl.BlockSpec(memory_space=pl.ANY)] * 8,
        out_specs=[pl.BlockSpec(memory_space=pltpu.VMEM)] * 4,
        out_shape=outs,
        scratch_shapes=[
            pltpu.VMEM((tokens, depth), jnp.bfloat16),
            pltpu.VMEM((tokens, args[1].shape[2]), jnp.bfloat16),
            *[pltpu.VMEM(a.shape, a.dtype) for a in args[4:]],
            pltpu.VMEM((tokens, width), jnp.float32),
            pltpu.VMEM((tokens, width), jnp.float32),
            pltpu.SemaphoreType.DMA((2 * n + 6,)),
        ],
        compiler_params=pltpu.CompilerParams(vmem_limit_bytes=WIDE),
        cost_estimate=pl.CostEstimate(
            flops=2 * tokens * (depth + args[1].shape[2]) * width,
            bytes_accessed=2 * sum(a.size for a in args),
            transcendentals=0,
        ),
    )(*args)


def grad_kernel(n, ya_ref, yb_ref, xa_ref, xb_ref, keep_ref, send_ref, grad_ref):
    core = lax.axis_index("c")
    rows = HALF // 2
    mine = pl.ds(pl.multiple_of(core * rows, rows), rows)
    other = pl.ds(pl.multiple_of((1 - core) * rows, rows), rows)
    for s in range(n):
        grad_ref[...] = dot3(ya_ref[s] + yb_ref[s], xa_ref[s] + xb_ref[s], ((0,), (0,)))
        keep_ref[s] = grad_ref[mine]
        send_ref[s] = grad_ref[other]


def gradient(ya, yb, xa, xb):
    n = ya.shape[0]
    out = jax.ShapeDtypeStruct((n, HALF // 2, HALF), jnp.float32)
    return pl.pallas_call(
        functools.partial(grad_kernel, n),
        out_shape=[out, out],
        scratch_shapes=[pltpu.VMEM((HALF, HALF), jnp.float32)],
        compiler_params=pltpu.CompilerParams(vmem_limit_bytes=LIMIT),
        cost_estimate=pl.CostEstimate(
            flops=6 * ya.size * HALF, bytes_accessed=16 * ya.size, transcendentals=0
        ),
    )(ya, yb, xa, xb)


def score_kernel(four_ref, rest_ref, t0_ref, t1_ref, t2_ref, t3_ref, out_ref):
    x, z = lax.axis_index("x"), lax.axis_index("z")
    queries = [four_ref.at[i] for i in range(4)] + [rest_ref.at[i] for i in range(4)]
    lane = lax.broadcasted_iota(jnp.int32, (1, HALF), 1)
    for d, trains in enumerate((t0_ref, t1_ref, t2_ref, t3_ref)):
        row = jnp.zeros((1, HALF), jnp.float32)
        for query, by in zip(queries, AT_Z):
            place = x * 8 + jnp.bitwise_xor(z, by)
            for s in range(3):
                total = jnp.sum((query[...] * trains[s]).reshape(-1, 8, HALF), axis=0)
                total = jnp.sum(jnp.sum(total, axis=0, keepdims=True), axis=1, keepdims=True)
                row = jnp.where(lane == place + 32 * s, total, row)
        home = pl.multiple_of(jnp.bitwise_xor(x, d) * 8, 8)
        out_ref[pl.ds(home, 8), :] = jnp.broadcast_to(row, (8, HALF))


def score(four, rest, trains):
    return pl.pallas_call(
        score_kernel,
        out_shape=jax.ShapeDtypeStruct((32, HALF), jnp.float32),
        compiler_params=pltpu.CompilerParams(vmem_limit_bytes=LIMIT),
        cost_estimate=pl.CostEstimate(flops=2 * 96 * 8192, bytes_accessed=2**20, transcendentals=0),
    )(four, rest, *trains)


def finish_kernel(scale, parts_ref, out_ref):
    total = jnp.sum(parts_ref[...], axis=0, keepdims=True) * scale
    for s in range(3):
        out_ref[s : s + 1, :] = total[:, 32 * s : 32 * s + 32]


def finish(parts, scale):
    return pl.pallas_call(
        functools.partial(finish_kernel, scale),
        out_shape=jax.ShapeDtypeStruct((3, 32), jnp.float32),
        compiler_params=pltpu.CompilerParams(vmem_limit_bytes=LIMIT),
    )(parts).T


def body(
    train_inputs,
    train_grads_out,
    query_inputs,
    query_grads_out,
    proj_in,
    proj_out,
    out_inverse,
    in_inverse,
):
    length = train_inputs.shape[1]
    width = proj_in.shape[1]

    q_keep, q_send, keep, send = project(
        train_inputs, train_grads_out, query_inputs, query_grads_out, proj_in, proj_out, out_inverse, in_inverse
    )
    got = lax.ppermute(q_send, "c", CORES)
    y_got = lax.ppermute(q_keep[0] + got[0], "y", PAIRS_A)
    x_got = lax.ppermute(q_keep[1] + got[1], "y", PAIRS_B)
    y_half = (q_keep[2] + got[2]) + y_got
    x_half = (q_keep[3] + got[3]) + x_got

    got = lax.ppermute(after(send, got), "c", CORES)
    y_away, x_away = keep[0] + got[0], keep[1] + got[1]
    y_half, x_half = after((y_half, x_half), y_away)
    y_rest = lax.ppermute(y_half, "y", PAIRS_B)
    x_rest = lax.ppermute(x_half, "y", PAIRS_A)
    y_got = lax.ppermute(y_away, "y", PAIRS_A)
    x_got = lax.ppermute(x_away, "y", PAIRS_B)

    query, query_send = gradient(y_half, y_rest, x_half, x_rest)
    y_half = (keep[2] + got[2]) + y_got
    x_half = (keep[3] + got[3]) + x_got
    query = after(query + lax.ppermute(query_send, "c", CORES), (y_half, x_half))
    y_rest = lax.ppermute(y_half, "y", PAIRS_B)
    x_rest = lax.ppermute(x_half, "y", PAIRS_A)

    two = jnp.concatenate([query, across(query, "z", 7)], 0)
    four = jnp.concatenate([two, across(two, "z", 2)], 0)
    rest = across(four, "z", 1)
    keep, send = gradient(y_half, y_rest, x_half, x_rest)
    train = keep + lax.ppermute(send, "c", CORES)
    trains = [train] + [across(train, "x", bits) for bits in (1, 2, 3)]

    parts = lax.all_to_all(score(four, rest, trains), ("x", "y", "c"), 0, 0, tiled=True)
    return finish(parts, 1.0 / (length * width))


def solution(mesh):
    devices = Mesh(mesh.devices.reshape(4, 8, 4, 2), ("x", "z", "y", "c"))
    dp, mp = ("x", "z"), ("y", "c")
    return jax.shard_map(
        body,
        mesh=devices,
        in_specs=(
            P(dp, None, mp),
            P(dp, None, mp),
            P(dp, None, mp),
            P(dp, None, mp),
            P(mp, None),
            P(mp, None),
            P(),
            P(),
        ),
        out_specs=P(None, dp),
        check_vma=False,
    )
```

time: 79.1 us -> 70.2 us (0.89); the launches traced: 78.1 us -> 70 us
  blocking collectives: 0 us -> 15.6 us
  waiting for transfers between devices: 27.9 us -> 14.3 us
  matrix products: 12.1 us -> 0 us
  Pallas kernels: 0 us -> 11.4 us
  starting transfers between devices: 30.3 us -> 25.5 us
  local copies, waits for them, and re-layouts: 2.53 us -> 0.02 us
  other arithmetic: 4.87 us -> 3.11 us
    all_to_all x0 -> x1, blocking collectives: none -> 15.6 us  [body(): lax.all_to_all(score(four, rest, trains), ('x', 'y', 'c'), 0, 0, tiled=True)]
    dot_general x8 -> x0, matrix products: 12.1 us -> none  [the longest x4 8.69 us: project(): jnp.einsum('slk,kr->slr', acts, weights, preferred_element_type=jnp.float32)]
    pallas_call x0 -> x5, Pallas kernels: none -> 11.4 us  [the longest x1 9.77 us: project(): pl.pallas_call(project_kernel, in_specs=[pl.BlockSpec(memory_space=pl.ANY...]
    all_to_all x1 -> x0, starting transfers between devices: 9.77 us -> none  [body(): got = lax.all_to_all(part, ('x', 'y', 'c'), 0, 0, tiled=True)]
    all_to_all x1 -> x0, waiting for transfers between devices: 7.33 us -> none  [body(): got = lax.all_to_all(part, ('x', 'y', 'c'), 0, 0, tiled=True)]
    ppermute x14 -> x18, waiting for transfers between devices: 20.6 us -> 14.3 us  [the longest x6 5.81 us: across(): return lax.ppermute(value, axis, [(i, i ^ bits) for i in range(size)])]
    ppermute x14 -> x18, starting transfers between devices: 20.6 us -> 25.5 us  [the longest x6 11.6 us: across(): return lax.ppermute(value, axis, [(i, i ^ bits) for i in range(size)])]
    select_n x6 -> x0, other arithmetic: 1.99 us -> none  [the longest x5 1.97 us: halves(): return (jnp.where(swap, second, first), jnp.where(swap, first, second))]
  transfers between devices with their start and end apart: 15 -> 18, of which waited for: 8 -> 8; matrix products, arithmetic and copies ran while one was open for 12% -> 4% of each run, Pallas kernels for 0% -> 1%
where the time goes in v2:
time: 70.2 us; the launch traced here: 70 us
  starting transfers between devices  25.5 us (36%)
  blocking collectives  15.6 us (22%)
  waiting for transfers between devices  14.3 us (20%)
  Pallas kernels  11.4 us (16%)
  other arithmetic  3.11 us (4%)
    all_to_all x1, blocking collectives, body(): lax.all_to_all(score(four, rest, trains), ('x', 'y', 'c'), 0, 0, tiled=True)  15.6 us
    ppermute x6, starting transfers between devices, across(): return lax.ppermute(value, axis, [(i, i ^ bits) for i in range(size)])  11.6 us
    pallas_call x1, Pallas kernels, project(): pl.pallas_call(project_kernel, in_specs=[pl.BlockSpec(memory_space=pl.ANY...  9.77 us
    ppermute x6, waiting for transfers between devices, across(): return lax.ppermute(value, axis, [(i, i ^ bits) for i in range(size)])  5.81 us
    ppermute x2, waiting for transfers between devices, body(): y_rest = lax.ppermute(y_half, 'y', PAIRS_B)  5.4 us
    ppermute x1, starting transfers between devices, body(): got = lax.ppermute(q_send, 'c', CORES)  3.32 us
    ppermute x1, starting transfers between devices, body(): train = keep + lax.ppermute(send, 'c', CORES)  2.24 us
    ppermute x2, starting transfers between devices, body(): y_rest = lax.ppermute(y_half, 'y', PAIRS_B)  2.23 us
  transfers between devices with their start and end apart: 18, of which 8 were waited for; matrix products, arithmetic and copies ran while one was open for 4% of the time, Pallas kernels for 1%

profile of v2, /device:TPU:1, one launch (start us, length us, event | category | flops | bytes accessed | tf_op | source)
XLA Modules:
  0.0 70.0 jit_solution(15131593579502032518)
XLA Ops:
  0.0 9.8 %shard_map.82 = (f32[4,1,160,128]{3,2,1,0:T(8,128)}, f32[4,1,160,128]{3,2,1,0:T(8,128)}, f32[4,3,160,128]{3,2,1,0:T(8,128)}, f32[4,3,160,128]{3,2,1,0:T(8,128)}) custom-call(bf16[3,320,3456]{2,1,0:T(8,128)(2,1)} %refs_0_.1, bf16[3,320,640]{2,1,0:T(8,128)(2,1)} %refs_1_.1, bf16[1,320,3456]{2,1,0:T(8,128)(2,1)} %refs_2_.1, bf16[1,320,640]{2,1,0:T(8,128)(2,1)} %refs_3_.1, ...), custom_call_target="tpu_custom_call" | custom-call | flops 2684354560 | bytes 12845056 | tf_op jit(solution)/shard_map/pallas_call | solution.py:83
  9.8 3.3 %collective-permute-start = (f32[4,1,160,128]{3,2,1,0:T(8,128)}, f32[4,1,160,128]{3,2,1,0:T(8,128)S(1)}, u32[]{:S(2)}, u32[]{:S(2)}) collective-permute-start(f32[4,1,160,128]{3,2,1,0:T(8,128)} %get-tuple-element.18), channel_id=1, source_target_pairs={{0,1},{1,0},{2,3},{3,2},{4,5},{5,4},{6,7},{7,6},{8,9},{9,8},{10,11... | collective-permute-start | bytes 983048 | tf_op jit(solution)/shard_map/ppermute | solution.py:185
  13.1 1.5 %collective-permute-done = f32[4,1,160,128]{3,2,1,0:T(8,128)S(1)} collective-permute-done((f32[4,1,160,128]{3,2,1,0:T(8,128)}, f32[4,1,160,128]{3,2,1,0:T(8,128)S(1)}, u32[]{:S(2)}, u32[]{:S(2)}) %collective-permute-start) | collective-permute-done | bytes 327712 | tf_op jit(solution)/shard_map/ppermute | solution.py:185
  14.6 0.4 collective-permute-start.3
  14.9 0.9 %fusion.6 = (f32[1,160,128]{2,1,0:T(8,128)S(1)}, f32[1,160,128]{2,1,0:T(8,128)S(1)}) fusion(f32[4,1,160,128]{3,2,1,0:T(8,128)S(1)} %collective-permute-done, f32[4,1,160,128]{3,2,1,0:T(8,128)} %get-tuple-element.17), kind=kLoop, calls=%fused_computation.11 | loop fusion | flops 40960 | bytes 491520 | tf_op jit(solution)/shard_map/add | solution.py:187
  15.9 1.1 %collective-permute-start.2 = (f32[1,160,128]{2,1,0:T(8,128)S(1)}, f32[1,160,128]{2,1,0:T(8,128)S(1)}, u32[]{:S(2)}, u32[]{:S(2)}) collective-permute-start(f32[1,160,128]{2,1,0:T(8,128)S(1)} %get-tuple-element.35), channel_id=1, source_target_pairs={{0,6},{6,0},{2,4},{4,2},{1,7},{7,1},{3,5},{5,3},{8,14},{14,8},{10,... | collective-permute-start | bytes 245768 | tf_op jit(solution)/shard_map/ppermute | solution.py:187
  17.0 0.4 collective-permute-done.3
  17.3 1.1 %fusion = (f32[3,160,128]{2,1,0:T(8,128)S(1)}, f32[3,160,128]{2,1,0:T(8,128)S(1)}) fusion(f32[4,3,160,128]{3,2,1,0:T(8,128)S(1)} %collective-permute-done.3, f32[4,3,160,128]{3,2,1,0:T(8,128)} %get-tuple-element.19), kind=kLoop, calls=%fused_computation.1 | loop fusion | flops 122880 | bytes 1474560 | tf_op jit(solution)/shard_map/add | solution.py:192
  18.5 1.4 %collective-permute-start.8 = (f32[3,160,128]{2,1,0:T(8,128)S(1)}, f32[3,160,128]{2,1,0:T(8,128)S(1)}, u32[]{:S(2)}, u32[]{:S(2)}) collective-permute-start(f32[3,160,128]{2,1,0:T(8,128)S(1)} %get-tuple-element.31), channel_id=1, source_target_pairs={{0,6},{6,0},{2,4},{4,2},{1,7},{7,1},{3,5},{5,3},{8,14},{14,8},{10,... | collective-permute-start | bytes 737288 | tf_op jit(solution)/shard_map/ppermute | solution.py:197
  19.9 0.9 %collective-permute-start.7 = (f32[3,160,128]{2,1,0:T(8,128)S(1)}, f32[3,160,128]{2,1,0:T(8,128)S(1)}, u32[]{:S(2)}, u32[]{:S(2)}) collective-permute-start(f32[3,160,128]{2,1,0:T(8,128)S(1)} %get-tuple-element.32), channel_id=1, source_target_pairs={{0,2},{2,0},{4,6},{6,4},{1,3},{3,1},{5,7},{7,5},{8,10},{10,8},{12,... | collective-permute-start | bytes 737288 | tf_op jit(solution)/shard_map/ppermute | solution.py:196
  20.7 0.4 collective-permute-done.2
  21.1 1.0 %fusion.8 = (f32[1,160,128]{2,1,0:T(8,128)S(1)}, f32[1,160,128]{2,1,0:T(8,128)S(1)}) fusion(f32[1,160,128]{2,1,0:T(8,128)S(1)} %collective-permute-done.2, f32[4,1,160,128]{3,2,1,0:T(8,128)S(1)} %collective-permute-done, f32[4,1,160,128]{3,2,1,0:T(8,128)} %get-tuple-element.17, f32[1,160,128]{2,1,0:T(8,128)S(1)} %collective-permute-done.1), kind=kLoop, calls=%fused_computation.14 | loop fusion | flops 81920 | bytes 655360 | tf_op jit(solution)/shard_map/add | solution.py:189
  22.1 1.2 %collective-permute-start.4 = (f32[1,160,128]{2,1,0:T(8,128)S(1)}, f32[1,160,128]{2,1,0:T(8,128)S(1)}, u32[]{:S(2)}, u32[]{:S(2)}) collective-permute-start(f32[1,160,128]{2,1,0:T(8,128)S(1)} %get-tuple-element.22.ya_ref), channel_id=1, source_target_pairs={{0,6},{6,0},{2,4},{4,2},{1,7},{7,1},{3,5},{5,3},{8,14},{14,8},{10,... | collective-permute-start | bytes 245768 | tf_op jit(solution)/shard_map/ppermute | solution.py:194
  23.3 5.4 %collective-permute-done.4.yb_ref = f32[1,160,128]{2,1,0:T(8,128)S(1)} collective-permute-done((f32[1,160,128]{2,1,0:T(8,128)S(1)}, f32[1,160,128]{2,1,0:T(8,128)S(1)}, u32[]{:S(2)}, u32[]{:S(2)}) %collective-permute-start.4) | collective-permute-done | bytes 81952 | tf_op jit(solution)/shard_map/ppermute | solution.py:194
  28.7 0.3 shard_map.83
  29.0 1.4 %collective-permute-start.6 = (f32[1,64,128]{2,1,0:T(8,128)S(1)}, f32[1,64,128]{2,1,0:T(8,128)S(1)}, u32[]{:S(2)}, u32[]{:S(2)}) collective-permute-start(f32[1,64,128]{2,1,0:T(8,128)S(1)} %get-tuple-element.25), channel_id=1, source_target_pairs={{0,1},{1,0},{2,3},{3,2},{4,5},{5,4},{6,7},{7,6},{8,9},{9,8},{10,11... | collective-permute-start | bytes 98312 | tf_op jit(solution)/shard_map/ppermute | solution.py:202
  30.3 0.9 %collective-permute-done.6 = f32[1,64,128]{2,1,0:T(8,128)S(1)} collective-permute-done((f32[1,64,128]{2,1,0:T(8,128)S(1)}, f32[1,64,128]{2,1,0:T(8,128)S(1)}, u32[]{:S(2)}, u32[]{:S(2)}) %collective-permute-start.6) | collective-permute-done | bytes 32800 | tf_op jit(solution)/shard_map/ppermute | solution.py:202
  31.3 0.9 %collective-permute-start.13 = (f32[3,160,128]{2,1,0:T(8,128)S(1)}, f32[3,160,128]{2,1,0:T(8,128)S(1)}, u32[]{:S(2)}, u32[]{:S(2)}) collective-permute-start(f32[3,160,128]{2,1,0:T(8,128)S(1)} %get-tuple-element.29.xa_ref), channel_id=1, source_target_pairs={{0,2},{2,0},{4,6},{6,4},{1,3},{3,1},{5,7},{7,5},{8,10},{10,8},{12,... | collective-permute-start | bytes 737288 | tf_op jit(solution)/shard_map/ppermute | solution.py:204
  32.3 1.0 %collective-permute-start.12 = (f32[3,160,128]{2,1,0:T(8,128)S(1)}, f32[3,160,128]{2,1,0:T(8,128)S(1)}, u32[]{:S(2)}, u32[]{:S(2)}) collective-permute-start(f32[3,160,128]{2,1,0:T(8,128)S(1)} %get-tuple-element.30.ya_ref), channel_id=1, source_target_pairs={{0,6},{6,0},{2,4},{4,2},{1,7},{7,1},{3,5},{5,3},{8,14},{14,8},{10,... | collective-permute-start | bytes 737288 | tf_op jit(solution)/shard_map/ppermute | solution.py:203
  33.3 5.6 %collective-permute-start.9 = (f32[1,64,128]{2,1,0:T(8,128)S(1)}, f32[1,64,128]{2,1,0:T(8,128)S(1)}, u32[]{:S(2)}, u32[]{:S(2)}) collective-permute-start(f32[1,64,128]{2,1,0:T(8,128)S(1)} %add.110), channel_id=1, source_target_pairs={{0,56},{8,48},{16,40},{24,32},{32,24},{40,16},{48,8},{56,0},{1,57}... | collective-permute-start | bytes 98312 | tf_op jit(solution)/shard_map/ppermute | solution.py:21
  38.8 1.6 %collective-permute-done.9 = f32[1,64,128]{2,1,0:T(8,128)S(1)} collective-permute-done((f32[1,64,128]{2,1,0:T(8,128)S(1)}, f32[1,64,128]{2,1,0:T(8,128)S(1)}, u32[]{:S(2)}, u32[]{:S(2)}) %collective-permute-start.9) | collective-permute-done | bytes 32800 | tf_op jit(solution)/shard_map/ppermute | solution.py:21
  40.4 1.8 %collective-permute-start.10 = (f32[2,64,128]{2,1,0:T(8,128)S(1)}, f32[2,64,128]{2,1,0:T(8,128)S(1)}, u32[]{:S(2)}, u32[]{:S(2)}) collective-permute-start(f32[2,64,128]{2,1,0:T(8,128)S(1)} %pad_maximum_fusion), channel_id=1, source_target_pairs={{0,16},{8,24},{16,0},{24,8},{32,48},{40,56},{48,32},{56,40},{1,17}... | collective-permute-start | bytes 196616 | tf_op jit(solution)/shard_map/ppermute | solution.py:21
  42.2 0.4 shard_map.84
  42.6 2.2 %collective-permute-start.14 = (f32[3,64,128]{2,1,0:T(8,128)S(1)}, f32[3,64,128]{2,1,0:T(8,128)S(1)}, u32[]{:S(2)}, u32[]{:S(2)}) collective-permute-start(f32[3,64,128]{2,1,0:T(8,128)S(1)} %get-tuple-element.28), channel_id=1, source_target_pairs={{0,1},{1,0},{2,3},{3,2},{4,5},{5,4},{6,7},{7,6},{8,9},{9,8},{10,11... | collective-permute-start | bytes 294920 | tf_op jit(solution)/shard_map/ppermute | solution.py:210
  44.9 0.9 %collective-permute-start.11 = (f32[4,64,128]{2,1,0:T(8,128)S(1)}, f32[4,64,128]{2,1,0:T(8,128)S(1)}, u32[]{:S(2)}, u32[]{:S(2)}) collective-permute-start(f32[4,64,128]{2,1,0:T(8,128)S(1)} %constant_dynamic-update-slice_fusion.four_ref), channel_id=1, source_target_pairs={{0,8},{8,0},{16,24},{24,16},{32,40},{40,32},{48,56},{56,48},{1,9},... | collective-permute-start | bytes 393224 | tf_op jit(solution)/shard_map/ppermute | solution.py:21
  45.8 2.6 %collective-permute-start.17 = (f32[3,64,128]{2,1,0:T(8,128)S(1)}, f32[3,64,128]{2,1,0:T(8,128)S(1)}, u32[]{:S(2)}, u32[]{:S(2)}) collective-permute-start(f32[3,64,128]{2,1,0:T(8,128)S(1)} %add.119.t0_ref), channel_id=1, source_target_pairs={{0,192},{64,128},{128,64},{192,0},{1,193},{65,129},{129,65},{193,1... | collective-permute-start | bytes 294920 | tf_op jit(solution)/shard_map/ppermute | solution.py:21
  48.4 0.5 collective-permute-start.16
  49.2 1.8 %collective-permute-done.17.t3_ref = f32[3,64,128]{2,1,0:T(8,128)S(1)} collective-permute-done((f32[3,64,128]{2,1,0:T(8,128)S(1)}, f32[3,64,128]{2,1,0:T(8,128)S(1)}, u32[]{:S(2)}, u32[]{:S(2)}) %collective-permute-start.17) | collective-permute-done | bytes 98336 | tf_op jit(solution)/shard_map/ppermute | solution.py:21
  51.0 2.4 %collective-permute-done.16.t2_ref = f32[3,64,128]{2,1,0:T(8,128)S(1)} collective-permute-done((f32[3,64,128]{2,1,0:T(8,128)S(1)}, f32[3,64,128]{2,1,0:T(8,128)S(1)}, u32[]{:S(2)}, u32[]{:S(2)}) %collective-permute-start.16) | collective-permute-done | bytes 98336 | tf_op jit(solution)/shard_map/ppermute | solution.py:21
  53.4 0.4 shard_map.85
  53.7 15.6 %all_to_all.11 = f32[32,1,128]{2,1,0:T(1,128)S(1)} all-to-all(f32[32,1,128]{2,1,0:T(1,128)S(1)} %bitcast.30), channel_id=1, replica_groups=mesh['x'=4,'z'=8,'y'=4,'c'=2] {'x','y','c'}, dimensions={0} | all-to-all | bytes 32768 | tf_op jit(solution)/shard_map/all_to_all | solution.py:213
  69.3 0.7 shard_map.86
  (22 shorter events, 0.4 us)
Async XLA Ops:
  9.8 21.5 %copy-start = (f32[4,3,160,128]{3,2,1,0:T(8,128)S(1)}, f32[4,3,160,128]{3,2,1,0:T(8,128)}, u32[]{:S(2)}) copy-start(f32[4,3,160,128]{3,2,1,0:T(8,128)} %get-tuple-element.19) | copy-start | bytes 2949124
  9.8 4.8 %collective-permute-start = (f32[4,1,160,128]{3,2,1,0:T(8,128)}, f32[4,1,160,128]{3,2,1,0:T(8,128)S(1)}, u32[]{:S(2)}, u32[]{:S(2)}) collective-permute-start(f32[4,1,160,128]{3,2,1,0:T(8,128)} %get-tuple-element.18), channel_id=1, source_target_pairs={{0,1},{1,0},{2,3},{3,2},{4,5},{5,4},{6,7},{7,6},{8,9},{9,8},{10,11... | collective-permute-start | bytes 983048 | tf_op jit(solution)/shard_map/ppermute | solution.py:185
  14.6 2.8 %collective-permute-start.3 = (f32[4,3,160,128]{3,2,1,0:T(8,128)}, f32[4,3,160,128]{3,2,1,0:T(8,128)S(1)}, u32[]{:S(2)}, u32[]{:S(2)}) collective-permute-start(f32[4,3,160,128]{3,2,1,0:T(8,128)} %get-tuple-element.21), channel_id=1, source_target_pairs={{0,1},{1,0},{2,3},{3,2},{4,5},{5,4},{6,7},{7,6},{8,9},{9,8},{10,11... | collective-permute-start | bytes 2949128 | tf_op jit(solution)/shard_map/ppermute | solution.py:191
  15.9 5.2 %collective-permute-start.2 = (f32[1,160,128]{2,1,0:T(8,128)S(1)}, f32[1,160,128]{2,1,0:T(8,128)S(1)}, u32[]{:S(2)}, u32[]{:S(2)}) collective-permute-start(f32[1,160,128]{2,1,0:T(8,128)S(1)} %get-tuple-element.35), channel_id=1, source_target_pairs={{0,6},{6,0},{2,4},{4,2},{1,7},{7,1},{3,5},{5,3},{8,14},{14,8},{10,... | collective-permute-start | bytes 245768 | tf_op jit(solution)/shard_map/ppermute | solution.py:187
  17.0 4.1 %collective-permute-start.1 = (f32[1,160,128]{2,1,0:T(8,128)S(1)}, f32[1,160,128]{2,1,0:T(8,128)S(1)}, u32[]{:S(2)}, u32[]{:S(2)}) collective-permute-start(f32[1,160,128]{2,1,0:T(8,128)S(1)} %get-tuple-element.36), channel_id=1, source_target_pairs={{0,2},{2,0},{4,6},{6,4},{1,3},{3,1},{5,7},{7,5},{8,10},{10,8},{12,... | collective-permute-start | bytes 245768 | tf_op jit(solution)/shard_map/ppermute | solution.py:186
  18.5 12.8 %collective-permute-start.8 = (f32[3,160,128]{2,1,0:T(8,128)S(1)}, f32[3,160,128]{2,1,0:T(8,128)S(1)}, u32[]{:S(2)}, u32[]{:S(2)}) collective-permute-start(f32[3,160,128]{2,1,0:T(8,128)S(1)} %get-tuple-element.31), channel_id=1, source_target_pairs={{0,6},{6,0},{2,4},{4,2},{1,7},{7,1},{3,5},{5,3},{8,14},{14,8},{10,... | collective-permute-start | bytes 737288 | tf_op jit(solution)/shard_map/ppermute | solution.py:197
  19.9 11.4 %collective-permute-start.7 = (f32[3,160,128]{2,1,0:T(8,128)S(1)}, f32[3,160,128]{2,1,0:T(8,128)S(1)}, u32[]{:S(2)}, u32[]{:S(2)}) collective-permute-start(f32[3,160,128]{2,1,0:T(8,128)S(1)} %get-tuple-element.32), channel_id=1, source_target_pairs={{0,2},{2,0},{4,6},{6,4},{1,3},{3,1},{5,7},{7,5},{8,10},{10,8},{12,... | collective-permute-start | bytes 737288 | tf_op jit(solution)/shard_map/ppermute | solution.py:196
  22.1 6.6 %collective-permute-start.4 = (f32[1,160,128]{2,1,0:T(8,128)S(1)}, f32[1,160,128]{2,1,0:T(8,128)S(1)}, u32[]{:S(2)}, u32[]{:S(2)}) collective-permute-start(f32[1,160,128]{2,1,0:T(8,128)S(1)} %get-tuple-element.22.ya_ref), channel_id=1, source_target_pairs={{0,6},{6,0},{2,4},{4,2},{1,7},{7,1},{3,5},{5,3},{8,14},{14,8},{10,... | collective-permute-start | bytes 245768 | tf_op jit(solution)/shard_map/ppermute | solution.py:194
  23.3 5.4 %collective-permute-start.5 = (f32[1,160,128]{2,1,0:T(8,128)S(1)}, f32[1,160,128]{2,1,0:T(8,128)S(1)}, u32[]{:S(2)}, u32[]{:S(2)}) collective-permute-start(f32[1,160,128]{2,1,0:T(8,128)S(1)} %get-tuple-element.23.xa_ref), channel_id=1, source_target_pairs={{0,2},{2,0},{4,6},{6,4},{1,3},{3,1},{5,7},{7,5},{8,10},{10,8},{12,... | collective-permute-start | bytes 245768 | tf_op jit(solution)/shard_map/ppermute | solution.py:195
  29.0 2.2 %collective-permute-start.6 = (f32[1,64,128]{2,1,0:T(8,128)S(1)}, f32[1,64,128]{2,1,0:T(8,128)S(1)}, u32[]{:S(2)}, u32[]{:S(2)}) collective-permute-start(f32[1,64,128]{2,1,0:T(8,128)S(1)} %get-tuple-element.25), channel_id=1, source_target_pairs={{0,1},{1,0},{2,3},{3,2},{4,5},{5,4},{6,7},{7,6},{8,9},{9,8},{10,11... | collective-permute-start | bytes 98312 | tf_op jit(solution)/shard_map/ppermute | solution.py:202
  31.3 10.9 %collective-permute-start.13 = (f32[3,160,128]{2,1,0:T(8,128)S(1)}, f32[3,160,128]{2,1,0:T(8,128)S(1)}, u32[]{:S(2)}, u32[]{:S(2)}) collective-permute-start(f32[3,160,128]{2,1,0:T(8,128)S(1)} %get-tuple-element.29.xa_ref), channel_id=1, source_target_pairs={{0,2},{2,0},{4,6},{6,4},{1,3},{3,1},{5,7},{7,5},{8,10},{10,8},{12,... | collective-permute-start | bytes 737288 | tf_op jit(solution)/shard_map/ppermute | solution.py:204
  32.3 10.0 %collective-permute-start.12 = (f32[3,160,128]{2,1,0:T(8,128)S(1)}, f32[3,160,128]{2,1,0:T(8,128)S(1)}, u32[]{:S(2)}, u32[]{:S(2)}) collective-permute-start(f32[3,160,128]{2,1,0:T(8,128)S(1)} %get-tuple-element.30.ya_ref), channel_id=1, source_target_pairs={{0,6},{6,0},{2,4},{4,2},{1,7},{7,1},{3,5},{5,3},{8,14},{14,8},{10,... | collective-permute-start | bytes 737288 | tf_op jit(solution)/shard_map/ppermute | solution.py:203
  33.3 7.2 %collective-permute-start.9 = (f32[1,64,128]{2,1,0:T(8,128)S(1)}, f32[1,64,128]{2,1,0:T(8,128)S(1)}, u32[]{:S(2)}, u32[]{:S(2)}) collective-permute-start(f32[1,64,128]{2,1,0:T(8,128)S(1)} %add.110), channel_id=1, source_target_pairs={{0,56},{8,48},{16,40},{24,32},{32,24},{40,16},{48,8},{56,0},{1,57}... | collective-permute-start | bytes 98312 | tf_op jit(solution)/shard_map/ppermute | solution.py:21
  40.4 4.4 %collective-permute-start.10 = (f32[2,64,128]{2,1,0:T(8,128)S(1)}, f32[2,64,128]{2,1,0:T(8,128)S(1)}, u32[]{:S(2)}, u32[]{:S(2)}) collective-permute-start(f32[2,64,128]{2,1,0:T(8,128)S(1)} %pad_maximum_fusion), channel_id=1, source_target_pairs={{0,16},{8,24},{16,0},{24,8},{32,48},{40,56},{48,32},{56,40},{1,17}... | collective-permute-start | bytes 196616 | tf_op jit(solution)/shard_map/ppermute | solution.py:21
  42.6 3.2 %collective-permute-start.14 = (f32[3,64,128]{2,1,0:T(8,128)S(1)}, f32[3,64,128]{2,1,0:T(8,128)S(1)}, u32[]{:S(2)}, u32[]{:S(2)}) collective-permute-start(f32[3,64,128]{2,1,0:T(8,128)S(1)} %get-tuple-element.28), channel_id=1, source_target_pairs={{0,1},{1,0},{2,3},{3,2},{4,5},{5,4},{6,7},{7,6},{8,9},{9,8},{10,11... | collective-permute-start | bytes 294920 | tf_op jit(solution)/shard_map/ppermute | solution.py:210
  44.9 4.3 %collective-permute-start.11 = (f32[4,64,128]{2,1,0:T(8,128)S(1)}, f32[4,64,128]{2,1,0:T(8,128)S(1)}, u32[]{:S(2)}, u32[]{:S(2)}) collective-permute-start(f32[4,64,128]{2,1,0:T(8,128)S(1)} %constant_dynamic-update-slice_fusion.four_ref), channel_id=1, source_target_pairs={{0,8},{8,0},{16,24},{24,16},{32,40},{40,32},{48,56},{56,48},{1,9},... | collective-permute-start | bytes 393224 | tf_op jit(solution)/shard_map/ppermute | solution.py:21
  45.8 5.2 %collective-permute-start.17 = (f32[3,64,128]{2,1,0:T(8,128)S(1)}, f32[3,64,128]{2,1,0:T(8,128)S(1)}, u32[]{:S(2)}, u32[]{:S(2)}) collective-permute-start(f32[3,64,128]{2,1,0:T(8,128)S(1)} %add.119.t0_ref), channel_id=1, source_target_pairs={{0,192},{64,128},{128,64},{192,0},{1,193},{65,129},{129,65},{193,1... | collective-permute-start | bytes 294920 | tf_op jit(solution)/shard_map/ppermute | solution.py:21
  48.4 5.0 %collective-permute-start.16 = (f32[3,64,128]{2,1,0:T(8,128)S(1)}, f32[3,64,128]{2,1,0:T(8,128)S(1)}, u32[]{:S(2)}, u32[]{:S(2)}) collective-permute-start(f32[3,64,128]{2,1,0:T(8,128)S(1)} %add.119.t0_ref), channel_id=1, source_target_pairs={{0,128},{64,192},{128,0},{192,64},{1,129},{65,193},{129,1},{193,65... | collective-permute-start | bytes 294920 | tf_op jit(solution)/shard_map/ppermute | solution.py:21
  48.9 4.5 %collective-permute-start.15 = (f32[3,64,128]{2,1,0:T(8,128)S(1)}, f32[3,64,128]{2,1,0:T(8,128)S(1)}, u32[]{:S(2)}, u32[]{:S(2)}) collective-permute-start(f32[3,64,128]{2,1,0:T(8,128)S(1)} %add.119.t0_ref), channel_id=1, source_target_pairs={{0,64},{64,0},{128,192},{192,128},{1,65},{65,1},{129,193},{193,129... | collective-permute-start | bytes 294920 | tf_op jit(solution)/shard_map/ppermute | solution.py:21

commit v3 on v2

--- a/solution.py
+++ b/solution.py
@@ -127,11 +127,12 @@
     )(ya, yb, xa, xb)
 
 
-def score_kernel(four_ref, rest_ref, t0_ref, t1_ref, t2_ref, t3_ref, out_ref):
+def score_kernel(*refs):
+    pairs, trains_of, out_ref = refs[:4], refs[4:8], refs[8]
     x, z = lax.axis_index("x"), lax.axis_index("z")
-    queries = [four_ref.at[i] for i in range(4)] + [rest_ref.at[i] for i in range(4)]
+    queries = [pair.at[i] for pair in pairs for i in range(2)]
     lane = lax.broadcasted_iota(jnp.int32, (1, HALF), 1)
-    for d, trains in enumerate((t0_ref, t1_ref, t2_ref, t3_ref)):
+    for d, trains in enumerate(trains_of):
         row = jnp.zeros((1, HALF), jnp.float32)
         for query, by in zip(queries, AT_Z):
             place = x * 8 + jnp.bitwise_xor(z, by)
@@ -143,13 +144,13 @@
         out_ref[pl.ds(home, 8), :] = jnp.broadcast_to(row, (8, HALF))
 
 
-def score(four, rest, trains):
+def score(queries, trains):
     return pl.pallas_call(
         score_kernel,
         out_shape=jax.ShapeDtypeStruct((32, HALF), jnp.float32),
         compiler_params=pltpu.CompilerParams(vmem_limit_bytes=LIMIT),
         cost_estimate=pl.CostEstimate(flops=2 * 96 * 8192, bytes_accessed=2**20, transcendentals=0),
-    )(four, rest, *trains)
+    )(*queries, *trains)
 
 
 def finish_kernel(scale, parts_ref, out_ref):
@@ -204,13 +205,13 @@
     x_rest = lax.ppermute(x_half, "y", PAIRS_A)
 
     two = jnp.concatenate([query, across(query, "z", 7)], 0)
-    four = jnp.concatenate([two, across(two, "z", 2)], 0)
-    rest = across(four, "z", 1)
-    keep, send = gradient(y_half, y_rest, x_half, x_rest)
+    more = across(two, "z", 2)
+    keep, send = gradient(y_half, after(y_rest, two), x_half, x_rest)
     train = keep + lax.ppermute(send, "c", CORES)
     trains = [train] + [across(train, "x", bits) for bits in (1, 2, 3)]
-
-    parts = lax.all_to_all(score(four, rest, trains), ("x", "y", "c"), 0, 0, tiled=True)
+    queries = [two, more, across(after(two, more), "z", 1), across(more, "z", 1)]
+
+    parts = lax.all_to_all(score(queries, trains), ("x", "y", "c"), 0, 0, tiled=True)
     return finish(parts, 1.0 / (length * width))
 
 

time: 70.2 us -> 67.8 us (0.966)
  blocking collectives: 15.6 us -> 13.9 us
  waiting for transfers between devices: 14.3 us -> 13.5 us
    ppermute x6 -> x7, starting transfers between devices: 11.6 us -> 13.4 us  [across(): return lax.ppermute(value, axis, [(i, i ^ bits) for i in range(size)])]
    all_to_all x1, blocking collectives: 15.6 us -> 13.9 us  [body(): lax.all_to_all(score(queries, trains), ('x', 'y', 'c'), 0, 0, tiled=True)]
    ppermute x1, starting transfers between devices: 2.24 us -> 1.04 us  [body(): train = keep + lax.ppermute(send, 'c', CORES)]
    ppermute x2, starting transfers between devices: 0.95 us -> 0.01 us  [body(): x_rest = lax.ppermute(x_half, 'y', PAIRS_A)]
    ppermute x1, waiting for transfers between devices: 0.86 us -> 0.01 us  [body(): lax.ppermute(query_send, 'c', CORES)]
    ppermute x6 -> x7, waiting for transfers between devices: 5.81 us -> 5.66 us  [across(): return lax.ppermute(value, axis, [(i, i ^ bits) for i in range(size)])]
  transfers between devices with their start and end apart: 18 -> 19, of which waited for: 8 -> 8; matrix products, arithmetic and copies ran while one was open for 4% -> 5% of each run, Pallas kernels for 1% -> 0%
where the time goes in v3:
time: 67.8 us; the launch traced here: 67.6 us
  starting transfers between devices  25.5 us (38%)
  blocking collectives  13.9 us (21%)
  waiting for transfers between devices  13.5 us (20%)
  Pallas kernels  11.4 us (17%)
  other arithmetic  3.11 us (5%)
    all_to_all x1, blocking collectives, body(): lax.all_to_all(score(queries, trains), ('x', 'y', 'c'), 0, 0, tiled=True)  13.9 us
    ppermute x7, starting transfers between devices, across(): return lax.ppermute(value, axis, [(i, i ^ bits) for i in range(size)])  13.4 us
    pallas_call x1, Pallas kernels, project(): pl.pallas_call(project_kernel, in_specs=[pl.BlockSpec(memory_space=pl.ANY...  9.76 us
    ppermute x7, waiting for transfers between devices, across(): return lax.ppermute(value, axis, [(i, i ^ bits) for i in range(size)])  5.66 us
    ppermute x2, waiting for transfers between devices, body(): y_rest = lax.ppermute(y_half, 'y', PAIRS_B)  5.64 us
    ppermute x1, starting transfers between devices, body(): got = lax.ppermute(q_send, 'c', CORES)  3.32 us
    ppermute x2, starting transfers between devices, body(): y_rest = lax.ppermute(y_half, 'y', PAIRS_B)  2.68 us
    ppermute x1, waiting for transfers between devices, body(): got = lax.ppermute(q_send, 'c', CORES)  1.47 us
  transfers between devices with their start and end apart: 19, of which 8 were waited for; matrix products, arithmetic and copies ran while one was open for 5% of the time, Pallas kernels for 0%

profile of v3, /device:TPU:1, one launch (start us, length us, event | category | flops | bytes accessed | tf_op | source)
XLA Modules:
  0.0 67.6 jit_solution(15767662632019378278)
XLA Ops:
  0.0 9.8 %shard_map.82 = (f32[4,1,160,128]{3,2,1,0:T(8,128)}, f32[4,1,160,128]{3,2,1,0:T(8,128)}, f32[4,3,160,128]{3,2,1,0:T(8,128)}, f32[4,3,160,128]{3,2,1,0:T(8,128)}) custom-call(bf16[3,320,3456]{2,1,0:T(8,128)(2,1)} %refs_0_.1, bf16[3,320,640]{2,1,0:T(8,128)(2,1)} %refs_1_.1, bf16[1,320,3456]{2,1,0:T(8,128)(2,1)} %refs_2_.1, bf16[1,320,640]{2,1,0:T(8,128)(2,1)} %refs_3_.1, ...), custom_call_target="tpu_custom_call" | custom-call | flops 2684354560 | bytes 12845056 | tf_op jit(solution)/shard_map/pallas_call | solution.py:83
  9.8 3.3 %collective-permute-start = (f32[4,1,160,128]{3,2,1,0:T(8,128)}, f32[4,1,160,128]{3,2,1,0:T(8,128)S(1)}, u32[]{:S(2)}, u32[]{:S(2)}) collective-permute-start(f32[4,1,160,128]{3,2,1,0:T(8,128)} %get-tuple-element.20), channel_id=1, source_target_pairs={{0,1},{1,0},{2,3},{3,2},{4,5},{5,4},{6,7},{7,6},{8,9},{9,8},{10,11... | collective-permute-start | bytes 983048 | tf_op jit(solution)/shard_map/ppermute | solution.py:186
  13.1 1.5 %collective-permute-done = f32[4,1,160,128]{3,2,1,0:T(8,128)S(1)} collective-permute-done((f32[4,1,160,128]{3,2,1,0:T(8,128)}, f32[4,1,160,128]{3,2,1,0:T(8,128)S(1)}, u32[]{:S(2)}, u32[]{:S(2)}) %collective-permute-start) | collective-permute-done | bytes 327712 | tf_op jit(solution)/shard_map/ppermute | solution.py:186
  14.6 0.4 collective-permute-start.3
  14.9 0.9 %fusion.6 = (f32[1,160,128]{2,1,0:T(8,128)S(1)}, f32[1,160,128]{2,1,0:T(8,128)S(1)}) fusion(f32[4,1,160,128]{3,2,1,0:T(8,128)S(1)} %collective-permute-done, f32[4,1,160,128]{3,2,1,0:T(8,128)} %get-tuple-element.19), kind=kLoop, calls=%fused_computation.11 | loop fusion | flops 40960 | bytes 491520 | tf_op jit(solution)/shard_map/add | solution.py:188
  15.9 1.1 %collective-permute-start.2 = (f32[1,160,128]{2,1,0:T(8,128)S(1)}, f32[1,160,128]{2,1,0:T(8,128)S(1)}, u32[]{:S(2)}, u32[]{:S(2)}) collective-permute-start(f32[1,160,128]{2,1,0:T(8,128)S(1)} %get-tuple-element.39), channel_id=1, source_target_pairs={{0,6},{6,0},{2,4},{4,2},{1,7},{7,1},{3,5},{5,3},{8,14},{14,8},{10,... | collective-permute-start | bytes 245768 | tf_op jit(solution)/shard_map/ppermute | solution.py:188
  17.0 0.4 collective-permute-done.3
  17.3 1.1 %fusion = (f32[3,160,128]{2,1,0:T(8,128)S(1)}, f32[3,160,128]{2,1,0:T(8,128)S(1)}) fusion(f32[4,3,160,128]{3,2,1,0:T(8,128)S(1)} %collective-permute-done.3, f32[4,3,160,128]{3,2,1,0:T(8,128)} %get-tuple-element.21), kind=kLoop, calls=%fused_computation.1 | loop fusion | flops 122880 | bytes 1474560 | tf_op jit(solution)/shard_map/add | solution.py:193
  18.5 1.4 %collective-permute-start.8 = (f32[3,160,128]{2,1,0:T(8,128)S(1)}, f32[3,160,128]{2,1,0:T(8,128)S(1)}, u32[]{:S(2)}, u32[]{:S(2)}) collective-permute-start(f32[3,160,128]{2,1,0:T(8,128)S(1)} %get-tuple-element.35), channel_id=1, source_target_pairs={{0,6},{6,0},{2,4},{4,2},{1,7},{7,1},{3,5},{5,3},{8,14},{14,8},{10,... | collective-permute-start | bytes 737288 | tf_op jit(solution)/shard_map/ppermute | solution.py:198
  19.9 0.9 %collective-permute-start.7 = (f32[3,160,128]{2,1,0:T(8,128)S(1)}, f32[3,160,128]{2,1,0:T(8,128)S(1)}, u32[]{:S(2)}, u32[]{:S(2)}) collective-permute-start(f32[3,160,128]{2,1,0:T(8,128)S(1)} %get-tuple-element.36), channel_id=1, source_target_pairs={{0,2},{2,0},{4,6},{6,4},{1,3},{3,1},{5,7},{7,5},{8,10},{10,8},{12,... | collective-permute-start | bytes 737288 | tf_op jit(solution)/shard_map/ppermute | solution.py:197
  20.7 0.4 collective-permute-done.2
  21.1 1.0 %fusion.8 = (f32[1,160,128]{2,1,0:T(8,128)S(1)}, f32[1,160,128]{2,1,0:T(8,128)S(1)}) fusion(f32[1,160,128]{2,1,0:T(8,128)S(1)} %collective-permute-done.2, f32[4,1,160,128]{3,2,1,0:T(8,128)S(1)} %collective-permute-done, f32[4,1,160,128]{3,2,1,0:T(8,128)} %get-tuple-element.19, f32[1,160,128]{2,1,0:T(8,128)S(1)} %collective-permute-done.1), kind=kLoop, calls=%fused_computation.14 | loop fusion | flops 81920 | bytes 655360 | tf_op jit(solution)/shard_map/add | solution.py:190
  22.0 1.2 %collective-permute-start.4 = (f32[1,160,128]{2,1,0:T(8,128)S(1)}, f32[1,160,128]{2,1,0:T(8,128)S(1)}, u32[]{:S(2)}, u32[]{:S(2)}) collective-permute-start(f32[1,160,128]{2,1,0:T(8,128)S(1)} %get-tuple-element.24.ya_ref), channel_id=1, source_target_pairs={{0,6},{6,0},{2,4},{4,2},{1,7},{7,1},{3,5},{5,3},{8,14},{14,8},{10,... | collective-permute-start | bytes 245768 | tf_op jit(solution)/shard_map/ppermute | solution.py:195
  23.3 5.4 %collective-permute-done.4.yb_ref = f32[1,160,128]{2,1,0:T(8,128)S(1)} collective-permute-done((f32[1,160,128]{2,1,0:T(8,128)S(1)}, f32[1,160,128]{2,1,0:T(8,128)S(1)}, u32[]{:S(2)}, u32[]{:S(2)}) %collective-permute-start.4) | collective-permute-done | bytes 81952 | tf_op jit(solution)/shard_map/ppermute | solution.py:195
  28.7 0.3 shard_map.83
  29.0 1.4 %collective-permute-start.6 = (f32[1,64,128]{2,1,0:T(8,128)S(1)}, f32[1,64,128]{2,1,0:T(8,128)S(1)}, u32[]{:S(2)}, u32[]{:S(2)}) collective-permute-start(f32[1,64,128]{2,1,0:T(8,128)S(1)} %get-tuple-element.27), channel_id=1, source_target_pairs={{0,1},{1,0},{2,3},{3,2},{4,5},{5,4},{6,7},{7,6},{8,9},{9,8},{10,11... | collective-permute-start | bytes 98312 | tf_op jit(solution)/shard_map/ppermute | solution.py:203
  30.4 1.4 %collective-permute-start.13 = (f32[3,160,128]{2,1,0:T(8,128)S(1)}, f32[3,160,128]{2,1,0:T(8,128)S(1)}, u32[]{:S(2)}, u32[]{:S(2)}) collective-permute-start(f32[3,160,128]{2,1,0:T(8,128)S(1)} %get-tuple-element.34.ya_ref), channel_id=1, source_target_pairs={{0,6},{6,0},{2,4},{4,2},{1,7},{7,1},{3,5},{5,3},{8,14},{14,8},{10,... | collective-permute-start | bytes 737288 | tf_op jit(solution)/shard_map/ppermute | solution.py:204
  31.9 5.5 %collective-permute-start.9 = (f32[1,64,128]{2,1,0:T(8,128)S(1)}, f32[1,64,128]{2,1,0:T(8,128)S(1)}, u32[]{:S(2)}, u32[]{:S(2)}) collective-permute-start(f32[1,64,128]{2,1,0:T(8,128)S(1)} %add.110), channel_id=1, source_target_pairs={{0,56},{8,48},{16,40},{24,32},{32,24},{40,16},{48,8},{56,0},{1,57}... | collective-permute-start | bytes 98312 | tf_op jit(solution)/shard_map/ppermute | solution.py:21
  37.5 1.6 %collective-permute-done.9 = f32[1,64,128]{2,1,0:T(8,128)S(1)} collective-permute-done((f32[1,64,128]{2,1,0:T(8,128)S(1)}, f32[1,64,128]{2,1,0:T(8,128)S(1)}, u32[]{:S(2)}, u32[]{:S(2)}) %collective-permute-start.9) | collective-permute-done | bytes 32800 | tf_op jit(solution)/shard_map/ppermute | solution.py:21
  39.1 0.2 collective-permute-done.13.yb_ref
  39.3 0.4 shard_map.84
  39.7 1.0 %collective-permute-start.15 = (f32[3,64,128]{2,1,0:T(8,128)S(1)}, f32[3,64,128]{2,1,0:T(8,128)S(1)}, u32[]{:S(2)}, u32[]{:S(2)}) collective-permute-start(f32[3,64,128]{2,1,0:T(8,128)S(1)} %get-tuple-element.32), channel_id=1, source_target_pairs={{0,1},{1,0},{2,3},{3,2},{4,5},{5,4},{6,7},{7,6},{8,9},{9,8},{10,11... | collective-permute-start | bytes 294920 | tf_op jit(solution)/shard_map/ppermute | solution.py:210
  40.7 2.7 %collective-permute-start.10 = (f32[2,64,128]{2,1,0:T(8,128)S(1)}, f32[2,64,128]{2,1,0:T(8,128)S(1)}, u32[]{:S(2)}, u32[]{:S(2)}) collective-permute-start(f32[2,64,128]{2,1,0:T(8,128)S(1)} %constant_dynamic-update-slice_fusion.refs_0_), channel_id=1, source_target_pairs={{0,16},{8,24},{16,0},{24,8},{32,48},{40,56},{48,32},{56,40},{1,17}... | collective-permute-start | bytes 196616 | tf_op jit(solution)/shard_map/ppermute | solution.py:21
  43.4 2.7 %collective-permute-start.18 = (f32[3,64,128]{2,1,0:T(8,128)S(1)}, f32[3,64,128]{2,1,0:T(8,128)S(1)}, u32[]{:S(2)}, u32[]{:S(2)}) collective-permute-start(f32[3,64,128]{2,1,0:T(8,128)S(1)} %add.119.refs_4_), channel_id=1, source_target_pairs={{0,192},{64,128},{128,64},{192,0},{1,193},{65,129},{129,65},{193,1... | collective-permute-start | bytes 294920 | tf_op jit(solution)/shard_map/ppermute | solution.py:21
  46.1 0.5 collective-permute-start.17
  46.6 0.3 collective-permute-start.16
  46.9 1.6 %collective-permute-start.11 = (f32[2,64,128]{2,1,0:T(8,128)S(1)}, f32[2,64,128]{2,1,0:T(8,128)S(1)}, u32[]{:S(2)}, u32[]{:S(2)}) collective-permute-start(f32[2,64,128]{2,1,0:T(8,128)S(1)} %constant_dynamic-update-slice_fusion.refs_0_), channel_id=1, source_target_pairs={{0,8},{8,0},{16,24},{24,16},{32,40},{40,32},{48,56},{56,48},{1,9},... | collective-permute-start | bytes 196616 | tf_op jit(solution)/shard_map/ppermute | solution.py:21
  48.6 1.6 %collective-permute-done.11.refs_2_ = f32[2,64,128]{2,1,0:T(8,128)S(1)} collective-permute-done((f32[2,64,128]{2,1,0:T(8,128)S(1)}, f32[2,64,128]{2,1,0:T(8,128)S(1)}, u32[]{:S(2)}, u32[]{:S(2)}) %collective-permute-start.11) | collective-permute-done | bytes 65568 | tf_op jit(solution)/shard_map/ppermute | solution.py:21
  50.2 2.4 %collective-permute-done.12.refs_3_ = f32[2,64,128]{2,1,0:T(8,128)S(1)} collective-permute-done((f32[2,64,128]{2,1,0:T(8,128)S(1)}, f32[2,64,128]{2,1,0:T(8,128)S(1)}, u32[]{:S(2)}, u32[]{:S(2)}) %collective-permute-start.12) | collective-permute-done | bytes 65568 | tf_op jit(solution)/shard_map/ppermute | solution.py:21
  52.6 0.4 shard_map.85
  53.0 13.9 %all_to_all.11 = f32[32,1,128]{2,1,0:T(1,128)S(1)} all-to-all(f32[32,1,128]{2,1,0:T(1,128)S(1)} %bitcast.30), channel_id=1, replica_groups=mesh['x'=4,'z'=8,'y'=4,'c'=2] {'x','y','c'}, dimensions={0} | all-to-all | bytes 32768 | tf_op jit(solution)/shard_map/all_to_all | solution.py:214
  66.9 0.7 shard_map.86
  (22 shorter events, 0.2 us)
Async XLA Ops:
  9.8 20.6 %copy-start = (f32[4,3,160,128]{3,2,1,0:T(8,128)S(1)}, f32[4,3,160,128]{3,2,1,0:T(8,128)}, u32[]{:S(2)}) copy-start(f32[4,3,160,128]{3,2,1,0:T(8,128)} %get-tuple-element.21) | copy-start | bytes 2949124
  9.8 4.8 %collective-permute-start = (f32[4,1,160,128]{3,2,1,0:T(8,128)}, f32[4,1,160,128]{3,2,1,0:T(8,128)S(1)}, u32[]{:S(2)}, u32[]{:S(2)}) collective-permute-start(f32[4,1,160,128]{3,2,1,0:T(8,128)} %get-tuple-element.20), channel_id=1, source_target_pairs={{0,1},{1,0},{2,3},{3,2},{4,5},{5,4},{6,7},{7,6},{8,9},{9,8},{10,11... | collective-permute-start | bytes 983048 | tf_op jit(solution)/shard_map/ppermute | solution.py:186
  14.6 2.8 %collective-permute-start.3 = (f32[4,3,160,128]{3,2,1,0:T(8,128)}, f32[4,3,160,128]{3,2,1,0:T(8,128)S(1)}, u32[]{:S(2)}, u32[]{:S(2)}) collective-permute-start(f32[4,3,160,128]{3,2,1,0:T(8,128)} %get-tuple-element.23), channel_id=1, source_target_pairs={{0,1},{1,0},{2,3},{3,2},{4,5},{5,4},{6,7},{7,6},{8,9},{9,8},{10,11... | collective-permute-start | bytes 2949128 | tf_op jit(solution)/shard_map/ppermute | solution.py:192
  15.9 5.2 %collective-permute-start.2 = (f32[1,160,128]{2,1,0:T(8,128)S(1)}, f32[1,160,128]{2,1,0:T(8,128)S(1)}, u32[]{:S(2)}, u32[]{:S(2)}) collective-permute-start(f32[1,160,128]{2,1,0:T(8,128)S(1)} %get-tuple-element.39), channel_id=1, source_target_pairs={{0,6},{6,0},{2,4},{4,2},{1,7},{7,1},{3,5},{5,3},{8,14},{14,8},{10,... | collective-permute-start | bytes 245768 | tf_op jit(solution)/shard_map/ppermute | solution.py:188
  17.0 4.1 %collective-permute-start.1 = (f32[1,160,128]{2,1,0:T(8,128)S(1)}, f32[1,160,128]{2,1,0:T(8,128)S(1)}, u32[]{:S(2)}, u32[]{:S(2)}) collective-permute-start(f32[1,160,128]{2,1,0:T(8,128)S(1)} %get-tuple-element.40), channel_id=1, source_target_pairs={{0,2},{2,0},{4,6},{6,4},{1,3},{3,1},{5,7},{7,5},{8,10},{10,8},{12,... | collective-permute-start | bytes 245768 | tf_op jit(solution)/shard_map/ppermute | solution.py:187
  18.5 11.9 %collective-permute-start.8 = (f32[3,160,128]{2,1,0:T(8,128)S(1)}, f32[3,160,128]{2,1,0:T(8,128)S(1)}, u32[]{:S(2)}, u32[]{:S(2)}) collective-permute-start(f32[3,160,128]{2,1,0:T(8,128)S(1)} %get-tuple-element.35), channel_id=1, source_target_pairs={{0,6},{6,0},{2,4},{4,2},{1,7},{7,1},{3,5},{5,3},{8,14},{14,8},{10,... | collective-permute-start | bytes 737288 | tf_op jit(solution)/shard_map/ppermute | solution.py:198
  19.9 10.5 %collective-permute-start.7 = (f32[3,160,128]{2,1,0:T(8,128)S(1)}, f32[3,160,128]{2,1,0:T(8,128)S(1)}, u32[]{:S(2)}, u32[]{:S(2)}) collective-permute-start(f32[3,160,128]{2,1,0:T(8,128)S(1)} %get-tuple-element.36), channel_id=1, source_target_pairs={{0,2},{2,0},{4,6},{6,4},{1,3},{3,1},{5,7},{7,5},{8,10},{10,8},{12,... | collective-permute-start | bytes 737288 | tf_op jit(solution)/shard_map/ppermute | solution.py:197
  22.0 6.6 %collective-permute-start.4 = (f32[1,160,128]{2,1,0:T(8,128)S(1)}, f32[1,160,128]{2,1,0:T(8,128)S(1)}, u32[]{:S(2)}, u32[]{:S(2)}) collective-permute-start(f32[1,160,128]{2,1,0:T(8,128)S(1)} %get-tuple-element.24.ya_ref), channel_id=1, source_target_pairs={{0,6},{6,0},{2,4},{4,2},{1,7},{7,1},{3,5},{5,3},{8,14},{14,8},{10,... | collective-permute-start | bytes 245768 | tf_op jit(solution)/shard_map/ppermute | solution.py:195
  23.3 5.4 %collective-permute-start.5 = (f32[1,160,128]{2,1,0:T(8,128)S(1)}, f32[1,160,128]{2,1,0:T(8,128)S(1)}, u32[]{:S(2)}, u32[]{:S(2)}) collective-permute-start(f32[1,160,128]{2,1,0:T(8,128)S(1)} %get-tuple-element.25.xa_ref), channel_id=1, source_target_pairs={{0,2},{2,0},{4,6},{6,4},{1,3},{3,1},{5,7},{7,5},{8,10},{10,8},{12,... | collective-permute-start | bytes 245768 | tf_op jit(solution)/shard_map/ppermute | solution.py:196
  29.0 2.9 %collective-permute-start.6 = (f32[1,64,128]{2,1,0:T(8,128)S(1)}, f32[1,64,128]{2,1,0:T(8,128)S(1)}, u32[]{:S(2)}, u32[]{:S(2)}) collective-permute-start(f32[1,64,128]{2,1,0:T(8,128)S(1)} %get-tuple-element.27), channel_id=1, source_target_pairs={{0,1},{1,0},{2,3},{3,2},{4,5},{5,4},{6,7},{7,6},{8,9},{9,8},{10,11... | collective-permute-start | bytes 98312 | tf_op jit(solution)/shard_map/ppermute | solution.py:203
  30.4 8.8 %collective-permute-start.13 = (f32[3,160,128]{2,1,0:T(8,128)S(1)}, f32[3,160,128]{2,1,0:T(8,128)S(1)}, u32[]{:S(2)}, u32[]{:S(2)}) collective-permute-start(f32[3,160,128]{2,1,0:T(8,128)S(1)} %get-tuple-element.34.ya_ref), channel_id=1, source_target_pairs={{0,6},{6,0},{2,4},{4,2},{1,7},{7,1},{3,5},{5,3},{8,14},{14,8},{10,... | collective-permute-start | bytes 737288 | tf_op jit(solution)/shard_map/ppermute | solution.py:204
  31.9 7.4 %collective-permute-start.14 = (f32[3,160,128]{2,1,0:T(8,128)S(1)}, f32[3,160,128]{2,1,0:T(8,128)S(1)}, u32[]{:S(2)}, u32[]{:S(2)}) collective-permute-start(f32[3,160,128]{2,1,0:T(8,128)S(1)} %get-tuple-element.33.xa_ref), channel_id=1, source_target_pairs={{0,2},{2,0},{4,6},{6,4},{1,3},{3,1},{5,7},{7,5},{8,10},{10,8},{12,... | collective-permute-start | bytes 737288 | tf_op jit(solution)/shard_map/ppermute | solution.py:205
  31.9 7.1 %collective-permute-start.9 = (f32[1,64,128]{2,1,0:T(8,128)S(1)}, f32[1,64,128]{2,1,0:T(8,128)S(1)}, u32[]{:S(2)}, u32[]{:S(2)}) collective-permute-start(f32[1,64,128]{2,1,0:T(8,128)S(1)} %add.110), channel_id=1, source_target_pairs={{0,56},{8,48},{16,40},{24,32},{32,24},{40,16},{48,8},{56,0},{1,57}... | collective-permute-start | bytes 98312 | tf_op jit(solution)/shard_map/ppermute | solution.py:21
  39.7 3.7 %collective-permute-start.15 = (f32[3,64,128]{2,1,0:T(8,128)S(1)}, f32[3,64,128]{2,1,0:T(8,128)S(1)}, u32[]{:S(2)}, u32[]{:S(2)}) collective-permute-start(f32[3,64,128]{2,1,0:T(8,128)S(1)} %get-tuple-element.32), channel_id=1, source_target_pairs={{0,1},{1,0},{2,3},{3,2},{4,5},{5,4},{6,7},{7,6},{8,9},{9,8},{10,11... | collective-permute-start | bytes 294920 | tf_op jit(solution)/shard_map/ppermute | solution.py:210
  40.7 6.2 %collective-permute-start.10 = (f32[2,64,128]{2,1,0:T(8,128)S(1)}, f32[2,64,128]{2,1,0:T(8,128)S(1)}, u32[]{:S(2)}, u32[]{:S(2)}) collective-permute-start(f32[2,64,128]{2,1,0:T(8,128)S(1)} %constant_dynamic-update-slice_fusion.refs_0_), channel_id=1, source_target_pairs={{0,16},{8,24},{16,0},{24,8},{32,48},{40,56},{48,32},{56,40},{1,17}... | collective-permute-start | bytes 196616 | tf_op jit(solution)/shard_map/ppermute | solution.py:21
  43.4 9.2 %collective-permute-start.18 = (f32[3,64,128]{2,1,0:T(8,128)S(1)}, f32[3,64,128]{2,1,0:T(8,128)S(1)}, u32[]{:S(2)}, u32[]{:S(2)}) collective-permute-start(f32[3,64,128]{2,1,0:T(8,128)S(1)} %add.119.refs_4_), channel_id=1, source_target_pairs={{0,192},{64,128},{128,64},{192,0},{1,193},{65,129},{129,65},{193,1... | collective-permute-start | bytes 294920 | tf_op jit(solution)/shard_map/ppermute | solution.py:21
  46.1 6.5 %collective-permute-start.17 = (f32[3,64,128]{2,1,0:T(8,128)S(1)}, f32[3,64,128]{2,1,0:T(8,128)S(1)}, u32[]{:S(2)}, u32[]{:S(2)}) collective-permute-start(f32[3,64,128]{2,1,0:T(8,128)S(1)} %add.119.refs_4_), channel_id=1, source_target_pairs={{0,128},{64,192},{128,0},{192,64},{1,129},{65,193},{129,1},{193,65... | collective-permute-start | bytes 294920 | tf_op jit(solution)/shard_map/ppermute | solution.py:21
  46.6 6.0 %collective-permute-start.16 = (f32[3,64,128]{2,1,0:T(8,128)S(1)}, f32[3,64,128]{2,1,0:T(8,128)S(1)}, u32[]{:S(2)}, u32[]{:S(2)}) collective-permute-start(f32[3,64,128]{2,1,0:T(8,128)S(1)} %add.119.refs_4_), channel_id=1, source_target_pairs={{0,64},{64,0},{128,192},{192,128},{1,65},{65,1},{129,193},{193,129... | collective-permute-start | bytes 294920 | tf_op jit(solution)/shard_map/ppermute | solution.py:21
  46.9 3.3 %collective-permute-start.11 = (f32[2,64,128]{2,1,0:T(8,128)S(1)}, f32[2,64,128]{2,1,0:T(8,128)S(1)}, u32[]{:S(2)}, u32[]{:S(2)}) collective-permute-start(f32[2,64,128]{2,1,0:T(8,128)S(1)} %constant_dynamic-update-slice_fusion.refs_0_), channel_id=1, source_target_pairs={{0,8},{8,0},{16,24},{24,16},{32,40},{40,32},{48,56},{56,48},{1,9},... | collective-permute-start | bytes 196616 | tf_op jit(solution)/shard_map/ppermute | solution.py:21
  48.5 4.1 %collective-permute-start.12 = (f32[2,64,128]{2,1,0:T(8,128)S(1)}, f32[2,64,128]{2,1,0:T(8,128)S(1)}, u32[]{:S(2)}, u32[]{:S(2)}) collective-permute-start(f32[2,64,128]{2,1,0:T(8,128)S(1)} %collective-permute-done.10.refs_1_), channel_id=1, source_target_pairs={{0,8},{8,0},{16,24},{24,16},{32,40},{40,32},{48,56},{56,48},{1,9},... | collective-permute-start | bytes 196616 | tf_op jit(solution)/shard_map/ppermute | solution.py:21

commit v4 on v3

--- a/solution.py
+++ b/solution.py
@@ -12,7 +12,7 @@
 CORES = [(0, 1), (1, 0)]
 HALF = 128
 LIMIT = 24 * 2**20
-WIDE = 58 * 2**20
+WIDE = 56 * 2**20
 AT_Z = (0, 7, 2, 5, 1, 6, 3, 4)
 
 
@@ -79,7 +79,7 @@
 def project(*args):
     n, length, depth = args[0].shape
     tokens, width = (n + 1) * length, args[4].shape[1]
-    outs = [jax.ShapeDtypeStruct((4, k, length // 2, HALF), jnp.float32) for k in (1, 1, n, n)]
+    outs = [pltpu.VMEM((4, k, length // 2, HALF), jnp.float32) for k in (1, 1, n, n)]
     return pl.pallas_call(
         project_kernel,
         in_specs=[pl.BlockSpec(memory_space=pl.ANY)] * 8,

time: 67.8 us -> 64.7 us (0.954)
  other arithmetic: 3.11 us -> 0.19 us
  waiting for transfers between devices: 13.5 us -> 15.9 us
  Pallas kernels: 11.4 us -> 9.91 us
  starting transfers between devices: 25.5 us -> 24.5 us
    pallas_call x1, Pallas kernels: 9.76 us -> 8.25 us  [project(): pl.pallas_call(project_kernel, in_specs=[pl.BlockSpec(memory_space=pl.ANY...]
    add x1, other arithmetic: 1.11 us -> 0.05 us  [body(): y_away, x_away = (keep[0] + got[0], keep[1] + got[1])]
    ppermute x1, waiting for transfers between devices: 0.37 us -> 1.43 us  [body(): x_got = lax.ppermute(q_keep[1] + got[1], 'y', PAIRS_B)]
    add x1, other arithmetic: 0.95 us -> 0.03 us  [body(): x_half = q_keep[3] + got[3] + x_got]
    add x1, other arithmetic: 0.94 us -> 0.02 us  [body(): x_got = lax.ppermute(q_keep[1] + got[1], 'y', PAIRS_B)]
    ppermute x2, waiting for transfers between devices: 5.64 us -> 6.46 us  [body(): y_rest = lax.ppermute(y_half, 'y', PAIRS_B)]
    ppermute x1, waiting for transfers between devices: 0.37 us -> 1.08 us  [body(): got = lax.ppermute(after(send, got), 'c', CORES)]
  transfers between devices with their start and end apart: 19 -> 19, of which waited for: 8 -> 8; matrix products, arithmetic and copies ran while one was open for 5% -> 0% of each run, Pallas kernels for 0% -> 0%
where the time goes in v4:
time: 64.7 us; the launch traced here: 64.6 us
  starting transfers between devices  24.5 us (38%)
  waiting for transfers between devices  15.9 us (25%)
  blocking collectives  14 us (22%)
  Pallas kernels  9.91 us (15%)
    all_to_all x1, blocking collectives, body(): lax.all_to_all(score(queries, trains), ('x', 'y', 'c'), 0, 0, tiled=True)  14 us
    ppermute x7, starting transfers between devices, across(): return lax.ppermute(value, axis, [(i, i ^ bits) for i in range(size)])  12.9 us
    pallas_call x1, Pallas kernels, project(): pl.pallas_call(project_kernel, in_specs=[pl.BlockSpec(memory_space=pl.ANY...  8.25 us
    ppermute x2, waiting for transfers between devices, body(): y_rest = lax.ppermute(y_half, 'y', PAIRS_B)  6.46 us
    ppermute x7, waiting for transfers between devices, across(): return lax.ppermute(value, axis, [(i, i ^ bits) for i in range(size)])  5.65 us
    ppermute x1, starting transfers between devices, body(): got = lax.ppermute(q_send, 'c', CORES)  3.31 us
    ppermute x2, starting transfers between devices, body(): y_rest = lax.ppermute(y_half, 'y', PAIRS_B)  2.78 us
    ppermute x1, waiting for transfers between devices, body(): x_got = lax.ppermute(q_keep[1] + got[1], 'y', PAIRS_B)  1.43 us
  transfers between devices with their start and end apart: 19, of which 8 were waited for; matrix products, arithmetic and copies ran while one was open for 0% of the time, Pallas kernels for 0%

profile of v4, /device:TPU:1, one launch (start us, length us, event | category | flops | bytes accessed | tf_op | source)
XLA Modules:
  0.0 64.6 jit_solution(6423298352986170386)
XLA Ops:
  0.0 8.2 %shard_map.82 = (f32[4,1,160,128]{3,2,1,0:T(8,128)S(1)}, f32[4,1,160,128]{3,2,1,0:T(8,128)S(1)}, f32[4,3,160,128]{3,2,1,0:T(8,128)S(1)}, f32[4,3,160,128]{3,2,1,0:T(8,128)S(1)}) custom-call(bf16[3,320,3456]{2,1,0:T(8,128)(2,1)} %refs_0_.1, bf16[3,320,640]{2,1,0:T(8,128)(2,1)} %refs_1_.1, bf16[1,320,3456]{2,1,0:T(8,128)(2,1)} %refs_2_.1, ...), custom_call_target="tpu_custom_call" | custom-call | flops 2684354560 | bytes 12845056 | tf_op jit(solution)/shard_map/pallas_call | solution.py:83
  8.3 3.3 %collective-permute-start = (f32[4,1,160,128]{3,2,1,0:T(8,128)S(1)}, f32[4,1,160,128]{3,2,1,0:T(8,128)S(1)}, u32[]{:S(2)}, u32[]{:S(2)}) collective-permute-start(f32[4,1,160,128]{3,2,1,0:T(8,128)S(1)} %get-tuple-element.20), channel_id=1, source_target_pairs={{0,1},{1,0},{2,3},{3,2},{4,5},{5,4},{6,7},{7,6},{8,9},{9,8},{10,11... | collective-permute-start | bytes 983048 | tf_op jit(solution)/shard_map/ppermute | solution.py:186
  11.6 1.3 %collective-permute-done = f32[4,1,160,128]{3,2,1,0:T(8,128)S(1)} collective-permute-done((f32[4,1,160,128]{3,2,1,0:T(8,128)S(1)}, f32[4,1,160,128]{3,2,1,0:T(8,128)S(1)}, u32[]{:S(2)}, u32[]{:S(2)}) %collective-permute-start) | collective-permute-done | bytes 327712 | tf_op jit(solution)/shard_map/ppermute | solution.py:186
  12.8 0.4 collective-permute-start.3
  13.2 1.1 %collective-permute-start.2 = (f32[1,160,128]{2,1,0:T(8,128)S(1)}, f32[1,160,128]{2,1,0:T(8,128)S(1)}, u32[]{:S(2)}, u32[]{:S(2)}) collective-permute-start(f32[1,160,128]{2,1,0:T(8,128)S(1)} %get-tuple-element.39), channel_id=1, source_target_pairs={{0,6},{6,0},{2,4},{4,2},{1,7},{7,1},{3,5},{5,3},{8,14},{14,8},{10,... | collective-permute-start | bytes 245768 | tf_op jit(solution)/shard_map/ppermute | solution.py:188
  14.3 1.1 %collective-permute-done.3 = f32[4,3,160,128]{3,2,1,0:T(8,128)S(1)} collective-permute-done((f32[4,3,160,128]{3,2,1,0:T(8,128)S(1)}, f32[4,3,160,128]{3,2,1,0:T(8,128)S(1)}, u32[]{:S(2)}, u32[]{:S(2)}) %collective-permute-start.3) | collective-permute-done | bytes 983072 | tf_op jit(solution)/shard_map/ppermute | solution.py:192
  15.4 0.1 fusion
  15.5 1.1 %collective-permute-start.8 = (f32[3,160,128]{2,1,0:T(8,128)S(1)}, f32[3,160,128]{2,1,0:T(8,128)S(1)}, u32[]{:S(2)}, u32[]{:S(2)}) collective-permute-start(f32[3,160,128]{2,1,0:T(8,128)S(1)} %get-tuple-element.35), channel_id=1, source_target_pairs={{0,6},{6,0},{2,4},{4,2},{1,7},{7,1},{3,5},{5,3},{8,14},{14,8},{10,... | collective-permute-start | bytes 737288 | tf_op jit(solution)/shard_map/ppermute | solution.py:198
  16.5 0.5 collective-permute-start.7
  17.0 1.4 %collective-permute-done.2 = f32[1,160,128]{2,1,0:T(8,128)S(1)} collective-permute-done((f32[1,160,128]{2,1,0:T(8,128)S(1)}, f32[1,160,128]{2,1,0:T(8,128)S(1)}, u32[]{:S(2)}, u32[]{:S(2)}) %collective-permute-start.2) | collective-permute-done | bytes 81952 | tf_op jit(solution)/shard_map/ppermute | solution.py:188
  18.5 1.2 %collective-permute-start.4 = (f32[1,160,128]{2,1,0:T(8,128)S(1)}, f32[1,160,128]{2,1,0:T(8,128)S(1)}, u32[]{:S(2)}, u32[]{:S(2)}) collective-permute-start(f32[1,160,128]{2,1,0:T(8,128)S(1)} %get-tuple-element.24.ya_ref), channel_id=1, source_target_pairs={{0,6},{6,0},{2,4},{4,2},{1,7},{7,1},{3,5},{5,3},{8,14},{14,8},{10,... | collective-permute-start | bytes 245768 | tf_op jit(solution)/shard_map/ppermute | solution.py:195
  19.7 6.0 %collective-permute-done.4.yb_ref = f32[1,160,128]{2,1,0:T(8,128)S(1)} collective-permute-done((f32[1,160,128]{2,1,0:T(8,128)S(1)}, f32[1,160,128]{2,1,0:T(8,128)S(1)}, u32[]{:S(2)}, u32[]{:S(2)}) %collective-permute-start.4) | collective-permute-done | bytes 81952 | tf_op jit(solution)/shard_map/ppermute | solution.py:195
  25.7 0.3 shard_map.83
  25.9 1.3 %collective-permute-start.6 = (f32[1,64,128]{2,1,0:T(8,128)S(1)}, f32[1,64,128]{2,1,0:T(8,128)S(1)}, u32[]{:S(2)}, u32[]{:S(2)}) collective-permute-start(f32[1,64,128]{2,1,0:T(8,128)S(1)} %get-tuple-element.27), channel_id=1, source_target_pairs={{0,1},{1,0},{2,3},{3,2},{4,5},{5,4},{6,7},{7,6},{8,9},{9,8},{10,11... | collective-permute-start | bytes 98312 | tf_op jit(solution)/shard_map/ppermute | solution.py:203
  27.2 0.1 fusion.2
  27.3 1.5 %collective-permute-start.13 = (f32[3,160,128]{2,1,0:T(8,128)S(1)}, f32[3,160,128]{2,1,0:T(8,128)S(1)}, u32[]{:S(2)}, u32[]{:S(2)}) collective-permute-start(f32[3,160,128]{2,1,0:T(8,128)S(1)} %get-tuple-element.34.ya_ref), channel_id=1, source_target_pairs={{0,6},{6,0},{2,4},{4,2},{1,7},{7,1},{3,5},{5,3},{8,14},{14,8},{10,... | collective-permute-start | bytes 737288 | tf_op jit(solution)/shard_map/ppermute | solution.py:204
  28.9 5.2 %collective-permute-start.9 = (f32[1,64,128]{2,1,0:T(8,128)S(1)}, f32[1,64,128]{2,1,0:T(8,128)S(1)}, u32[]{:S(2)}, u32[]{:S(2)}) collective-permute-start(f32[1,64,128]{2,1,0:T(8,128)S(1)} %add.110), channel_id=1, source_target_pairs={{0,56},{8,48},{16,40},{24,32},{32,24},{40,16},{48,8},{56,0},{1,57}... | collective-permute-start | bytes 98312 | tf_op jit(solution)/shard_map/ppermute | solution.py:21
  34.1 1.6 %collective-permute-done.9 = f32[1,64,128]{2,1,0:T(8,128)S(1)} collective-permute-done((f32[1,64,128]{2,1,0:T(8,128)S(1)}, f32[1,64,128]{2,1,0:T(8,128)S(1)}, u32[]{:S(2)}, u32[]{:S(2)}) %collective-permute-start.9) | collective-permute-done | bytes 32800 | tf_op jit(solution)/shard_map/ppermute | solution.py:21
  35.7 0.5 collective-permute-done.13.yb_ref
  36.2 0.4 shard_map.84
  36.5 1.2 %collective-permute-start.15 = (f32[3,64,128]{2,1,0:T(8,128)S(1)}, f32[3,64,128]{2,1,0:T(8,128)S(1)}, u32[]{:S(2)}, u32[]{:S(2)}) collective-permute-start(f32[3,64,128]{2,1,0:T(8,128)S(1)} %get-tuple-element.32), channel_id=1, source_target_pairs={{0,1},{1,0},{2,3},{3,2},{4,5},{5,4},{6,7},{7,6},{8,9},{9,8},{10,11... | collective-permute-start | bytes 294920 | tf_op jit(solution)/shard_map/ppermute | solution.py:210
  37.7 2.6 %collective-permute-start.10 = (f32[2,64,128]{2,1,0:T(8,128)S(1)}, f32[2,64,128]{2,1,0:T(8,128)S(1)}, u32[]{:S(2)}, u32[]{:S(2)}) collective-permute-start(f32[2,64,128]{2,1,0:T(8,128)S(1)} %constant_dynamic-update-slice_fusion.refs_0_), channel_id=1, source_target_pairs={{0,16},{8,24},{16,0},{24,8},{32,48},{40,56},{48,32},{56,40},{1,17}... | collective-permute-start | bytes 196616 | tf_op jit(solution)/shard_map/ppermute | solution.py:21
  40.3 2.7 %collective-permute-start.18 = (f32[3,64,128]{2,1,0:T(8,128)S(1)}, f32[3,64,128]{2,1,0:T(8,128)S(1)}, u32[]{:S(2)}, u32[]{:S(2)}) collective-permute-start(f32[3,64,128]{2,1,0:T(8,128)S(1)} %add.119.refs_4_), channel_id=1, source_target_pairs={{0,192},{64,128},{128,64},{192,0},{1,193},{65,129},{129,65},{193,1... | collective-permute-start | bytes 294920 | tf_op jit(solution)/shard_map/ppermute | solution.py:21
  43.0 0.5 collective-permute-start.17
  43.5 0.3 collective-permute-start.16
  43.8 1.6 %collective-permute-start.11 = (f32[2,64,128]{2,1,0:T(8,128)S(1)}, f32[2,64,128]{2,1,0:T(8,128)S(1)}, u32[]{:S(2)}, u32[]{:S(2)}) collective-permute-start(f32[2,64,128]{2,1,0:T(8,128)S(1)} %constant_dynamic-update-slice_fusion.refs_0_), channel_id=1, source_target_pairs={{0,8},{8,0},{16,24},{24,16},{32,40},{40,32},{48,56},{56,48},{1,9},... | collective-permute-start | bytes 196616 | tf_op jit(solution)/shard_map/ppermute | solution.py:21
  45.4 0.0 collective-permute-start.12
  45.5 1.6 %collective-permute-done.11.refs_2_ = f32[2,64,128]{2,1,0:T(8,128)S(1)} collective-permute-done((f32[2,64,128]{2,1,0:T(8,128)S(1)}, f32[2,64,128]{2,1,0:T(8,128)S(1)}, u32[]{:S(2)}, u32[]{:S(2)}) %collective-permute-start.11) | collective-permute-done | bytes 65568 | tf_op jit(solution)/shard_map/ppermute | solution.py:21
  47.1 2.4 %collective-permute-done.12.refs_3_ = f32[2,64,128]{2,1,0:T(8,128)S(1)} collective-permute-done((f32[2,64,128]{2,1,0:T(8,128)S(1)}, f32[2,64,128]{2,1,0:T(8,128)S(1)}, u32[]{:S(2)}, u32[]{:S(2)}) %collective-permute-start.12) | collective-permute-done | bytes 65568 | tf_op jit(solution)/shard_map/ppermute | solution.py:21
  49.5 0.4 shard_map.85
  49.9 14.0 %all_to_all.11 = f32[32,1,128]{2,1,0:T(1,128)S(1)} all-to-all(f32[32,1,128]{2,1,0:T(1,128)S(1)} %bitcast.30), channel_id=1, replica_groups=mesh['x'=4,'z'=8,'y'=4,'c'=2] {'x','y','c'}, dimensions={0} | all-to-all | bytes 32768 | tf_op jit(solution)/shard_map/all_to_all | solution.py:214
  63.9 0.7 %shard_map.86 = f32[3,32]{1,0:T(4,128)} custom-call(f32[32,128]{1,0:T(8,128)S(1)} %bitcast.29), custom_call_target="tpu_custom_call" | custom-call | tf_op jit(solution)/shard_map/pallas_call | solution.py:163
  (20 shorter events, 0.1 us)
Async XLA Ops:
  8.3 4.6 %collective-permute-start = (f32[4,1,160,128]{3,2,1,0:T(8,128)S(1)}, f32[4,1,160,128]{3,2,1,0:T(8,128)S(1)}, u32[]{:S(2)}, u32[]{:S(2)}) collective-permute-start(f32[4,1,160,128]{3,2,1,0:T(8,128)S(1)} %get-tuple-element.20), channel_id=1, source_target_pairs={{0,1},{1,0},{2,3},{3,2},{4,5},{5,4},{6,7},{7,6},{8,9},{9,8},{10,11... | collective-permute-start | bytes 983048 | tf_op jit(solution)/shard_map/ppermute | solution.py:186
  12.8 2.6 %collective-permute-start.3 = (f32[4,3,160,128]{3,2,1,0:T(8,128)S(1)}, f32[4,3,160,128]{3,2,1,0:T(8,128)S(1)}, u32[]{:S(2)}, u32[]{:S(2)}) collective-permute-start(f32[4,3,160,128]{3,2,1,0:T(8,128)S(1)} %get-tuple-element.23), channel_id=1, source_target_pairs={{0,1},{1,0},{2,3},{3,2},{4,5},{5,4},{6,7},{7,6},{8,9},{9,8},{10,11... | collective-permute-start | bytes 2949128 | tf_op jit(solution)/shard_map/ppermute | solution.py:192
  13.2 5.2 %collective-permute-start.2 = (f32[1,160,128]{2,1,0:T(8,128)S(1)}, f32[1,160,128]{2,1,0:T(8,128)S(1)}, u32[]{:S(2)}, u32[]{:S(2)}) collective-permute-start(f32[1,160,128]{2,1,0:T(8,128)S(1)} %get-tuple-element.39), channel_id=1, source_target_pairs={{0,6},{6,0},{2,4},{4,2},{1,7},{7,1},{3,5},{5,3},{8,14},{14,8},{10,... | collective-permute-start | bytes 245768 | tf_op jit(solution)/shard_map/ppermute | solution.py:188
  14.3 4.1 %collective-permute-start.1 = (f32[1,160,128]{2,1,0:T(8,128)S(1)}, f32[1,160,128]{2,1,0:T(8,128)S(1)}, u32[]{:S(2)}, u32[]{:S(2)}) collective-permute-start(f32[1,160,128]{2,1,0:T(8,128)S(1)} %get-tuple-element.40), channel_id=1, source_target_pairs={{0,2},{2,0},{4,6},{6,4},{1,3},{3,1},{5,7},{7,5},{8,10},{10,8},{12,... | collective-permute-start | bytes 245768 | tf_op jit(solution)/shard_map/ppermute | solution.py:187
  15.5 11.8 %collective-permute-start.8 = (f32[3,160,128]{2,1,0:T(8,128)S(1)}, f32[3,160,128]{2,1,0:T(8,128)S(1)}, u32[]{:S(2)}, u32[]{:S(2)}) collective-permute-start(f32[3,160,128]{2,1,0:T(8,128)S(1)} %get-tuple-element.35), channel_id=1, source_target_pairs={{0,6},{6,0},{2,4},{4,2},{1,7},{7,1},{3,5},{5,3},{8,14},{14,8},{10,... | collective-permute-start | bytes 737288 | tf_op jit(solution)/shard_map/ppermute | solution.py:198
  16.5 10.7 %collective-permute-start.7 = (f32[3,160,128]{2,1,0:T(8,128)S(1)}, f32[3,160,128]{2,1,0:T(8,128)S(1)}, u32[]{:S(2)}, u32[]{:S(2)}) collective-permute-start(f32[3,160,128]{2,1,0:T(8,128)S(1)} %get-tuple-element.36), channel_id=1, source_target_pairs={{0,2},{2,0},{4,6},{6,4},{1,3},{3,1},{5,7},{7,5},{8,10},{10,8},{12,... | collective-permute-start | bytes 737288 | tf_op jit(solution)/shard_map/ppermute | solution.py:197
  18.5 7.2 %collective-permute-start.4 = (f32[1,160,128]{2,1,0:T(8,128)S(1)}, f32[1,160,128]{2,1,0:T(8,128)S(1)}, u32[]{:S(2)}, u32[]{:S(2)}) collective-permute-start(f32[1,160,128]{2,1,0:T(8,128)S(1)} %get-tuple-element.24.ya_ref), channel_id=1, source_target_pairs={{0,6},{6,0},{2,4},{4,2},{1,7},{7,1},{3,5},{5,3},{8,14},{14,8},{10,... | collective-permute-start | bytes 245768 | tf_op jit(solution)/shard_map/ppermute | solution.py:195
  19.7 6.0 %collective-permute-start.5 = (f32[1,160,128]{2,1,0:T(8,128)S(1)}, f32[1,160,128]{2,1,0:T(8,128)S(1)}, u32[]{:S(2)}, u32[]{:S(2)}) collective-permute-start(f32[1,160,128]{2,1,0:T(8,128)S(1)} %get-tuple-element.25.xa_ref), channel_id=1, source_target_pairs={{0,2},{2,0},{4,6},{6,4},{1,3},{3,1},{5,7},{7,5},{8,10},{10,8},{12,... | collective-permute-start | bytes 245768 | tf_op jit(solution)/shard_map/ppermute | solution.py:196
  25.9 2.9 %collective-permute-start.6 = (f32[1,64,128]{2,1,0:T(8,128)S(1)}, f32[1,64,128]{2,1,0:T(8,128)S(1)}, u32[]{:S(2)}, u32[]{:S(2)}) collective-permute-start(f32[1,64,128]{2,1,0:T(8,128)S(1)} %get-tuple-element.27), channel_id=1, source_target_pairs={{0,1},{1,0},{2,3},{3,2},{4,5},{5,4},{6,7},{7,6},{8,9},{9,8},{10,11... | collective-permute-start | bytes 98312 | tf_op jit(solution)/shard_map/ppermute | solution.py:203
  27.3 8.8 %collective-permute-start.13 = (f32[3,160,128]{2,1,0:T(8,128)S(1)}, f32[3,160,128]{2,1,0:T(8,128)S(1)}, u32[]{:S(2)}, u32[]{:S(2)}) collective-permute-start(f32[3,160,128]{2,1,0:T(8,128)S(1)} %get-tuple-element.34.ya_ref), channel_id=1, source_target_pairs={{0,6},{6,0},{2,4},{4,2},{1,7},{7,1},{3,5},{5,3},{8,14},{14,8},{10,... | collective-permute-start | bytes 737288 | tf_op jit(solution)/shard_map/ppermute | solution.py:204
  28.9 7.3 %collective-permute-start.14 = (f32[3,160,128]{2,1,0:T(8,128)S(1)}, f32[3,160,128]{2,1,0:T(8,128)S(1)}, u32[]{:S(2)}, u32[]{:S(2)}) collective-permute-start(f32[3,160,128]{2,1,0:T(8,128)S(1)} %get-tuple-element.33.xa_ref), channel_id=1, source_target_pairs={{0,2},{2,0},{4,6},{6,4},{1,3},{3,1},{5,7},{7,5},{8,10},{10,8},{12,... | collective-permute-start | bytes 737288 | tf_op jit(solution)/shard_map/ppermute | solution.py:205
  28.9 6.8 %collective-permute-start.9 = (f32[1,64,128]{2,1,0:T(8,128)S(1)}, f32[1,64,128]{2,1,0:T(8,128)S(1)}, u32[]{:S(2)}, u32[]{:S(2)}) collective-permute-start(f32[1,64,128]{2,1,0:T(8,128)S(1)} %add.110), channel_id=1, source_target_pairs={{0,56},{8,48},{16,40},{24,32},{32,24},{40,16},{48,8},{56,0},{1,57}... | collective-permute-start | bytes 98312 | tf_op jit(solution)/shard_map/ppermute | solution.py:21
  36.5 3.7 %collective-permute-start.15 = (f32[3,64,128]{2,1,0:T(8,128)S(1)}, f32[3,64,128]{2,1,0:T(8,128)S(1)}, u32[]{:S(2)}, u32[]{:S(2)}) collective-permute-start(f32[3,64,128]{2,1,0:T(8,128)S(1)} %get-tuple-element.32), channel_id=1, source_target_pairs={{0,1},{1,0},{2,3},{3,2},{4,5},{5,4},{6,7},{7,6},{8,9},{9,8},{10,11... | collective-permute-start | bytes 294920 | tf_op jit(solution)/shard_map/ppermute | solution.py:210
  37.7 6.1 %collective-permute-start.10 = (f32[2,64,128]{2,1,0:T(8,128)S(1)}, f32[2,64,128]{2,1,0:T(8,128)S(1)}, u32[]{:S(2)}, u32[]{:S(2)}) collective-permute-start(f32[2,64,128]{2,1,0:T(8,128)S(1)} %constant_dynamic-update-slice_fusion.refs_0_), channel_id=1, source_target_pairs={{0,16},{8,24},{16,0},{24,8},{32,48},{40,56},{48,32},{56,40},{1,17}... | collective-permute-start | bytes 196616 | tf_op jit(solution)/shard_map/ppermute | solution.py:21
  40.3 9.2 %collective-permute-start.18 = (f32[3,64,128]{2,1,0:T(8,128)S(1)}, f32[3,64,128]{2,1,0:T(8,128)S(1)}, u32[]{:S(2)}, u32[]{:S(2)}) collective-permute-start(f32[3,64,128]{2,1,0:T(8,128)S(1)} %add.119.refs_4_), channel_id=1, source_target_pairs={{0,192},{64,128},{128,64},{192,0},{1,193},{65,129},{129,65},{193,1... | collective-permute-start | bytes 294920 | tf_op jit(solution)/shard_map/ppermute | solution.py:21
  43.0 6.5 %collective-permute-start.17 = (f32[3,64,128]{2,1,0:T(8,128)S(1)}, f32[3,64,128]{2,1,0:T(8,128)S(1)}, u32[]{:S(2)}, u32[]{:S(2)}) collective-permute-start(f32[3,64,128]{2,1,0:T(8,128)S(1)} %add.119.refs_4_), channel_id=1, source_target_pairs={{0,128},{64,192},{128,0},{192,64},{1,129},{65,193},{129,1},{193,65... | collective-permute-start | bytes 294920 | tf_op jit(solution)/shard_map/ppermute | solution.py:21
  43.5 6.0 %collective-permute-start.16 = (f32[3,64,128]{2,1,0:T(8,128)S(1)}, f32[3,64,128]{2,1,0:T(8,128)S(1)}, u32[]{:S(2)}, u32[]{:S(2)}) collective-permute-start(f32[3,64,128]{2,1,0:T(8,128)S(1)} %add.119.refs_4_), channel_id=1, source_target_pairs={{0,64},{64,0},{128,192},{192,128},{1,65},{65,1},{129,193},{193,129... | collective-permute-start | bytes 294920 | tf_op jit(solution)/shard_map/ppermute | solution.py:21
  43.8 3.3 %collective-permute-start.11 = (f32[2,64,128]{2,1,0:T(8,128)S(1)}, f32[2,64,128]{2,1,0:T(8,128)S(1)}, u32[]{:S(2)}, u32[]{:S(2)}) collective-permute-start(f32[2,64,128]{2,1,0:T(8,128)S(1)} %constant_dynamic-update-slice_fusion.refs_0_), channel_id=1, source_target_pairs={{0,8},{8,0},{16,24},{24,16},{32,40},{40,32},{48,56},{56,48},{1,9},... | collective-permute-start | bytes 196616 | tf_op jit(solution)/shard_map/ppermute | solution.py:21
  45.4 4.1 %collective-permute-start.12 = (f32[2,64,128]{2,1,0:T(8,128)S(1)}, f32[2,64,128]{2,1,0:T(8,128)S(1)}, u32[]{:S(2)}, u32[]{:S(2)}) collective-permute-start(f32[2,64,128]{2,1,0:T(8,128)S(1)} %collective-permute-done.10.refs_1_), channel_id=1, source_target_pairs={{0,8},{8,0},{16,24},{24,16},{32,40},{40,32},{48,56},{56,48},{1,9},... | collective-permute-start | bytes 196616 | tf_op jit(solution)/shard_map/ppermute | solution.py:21
